TPU v7x, 512 devices: a whole 4x8x8 slice. The times are simulated.
512 devices in a mesh: blk: 32 (over x, z_hi, core), col: 16 (over y, z_lo).
Axes of the slice: x: 4, y: 8, z: 8 (z_hi: 4, z_lo: 2; z = z_hi * 2 + z_lo), core: 2. Of those that a mesh axis runs over, the one named last changes fastest.
Arguments:
- features: float32 [8, 65536], P(None, ('blk', 'col')), may hold values from -6 to 6
- vectors: float32 [16, 65536], P(None, ('blk', 'col')), may hold values from -0.0234375 to 0.0234375
- lengthscales: float32 [8], replicated, may hold values from 0.7 to 3
- noise_var: float32 [65536], P(('blk', 'col')), may hold values from 0.5 to 64
- signal: float32 [1], replicated, may hold values from 0.5 to 2
Outputs:
- product: float32 [16, 65536], P(None, ('blk', 'col'))
All inputs are finite; a program needn't handle non-finite values.
Results may differ from a plain program's by a relative error of at most 0.00005.
Values sent between devices are 32-bit elements; how exact they have to be, the bound alone decides.
A program may use at most 64 MiB of HBM per device.

v0:
```python
import jax
import jax.numpy as jnp
from jax import lax
from jax.sharding import PartitionSpec as P

ROOT_FIVE = 2.23606797749979


def shifted(value, axis, steps):
    count = lax.axis_size(axis)
    pairs = [(source, (source + steps) % count) for source in range(count)]
    return lax.ppermute(value, axis, pairs)


def matern_tile(rows_x, rows_sq, cols_x, cols_sq):
    cross = lax.dot_general(
        rows_x,
        cols_x,
        (((0,), (0,)), ((), ())),
        precision=lax.Precision.HIGHEST,
        preferred_element_type=jnp.float32,
    )
    dist_sq = jnp.maximum(rows_sq[:, None] + cols_sq[None, :] - 2.0 * cross, 0.0)
    scaled_dist = ROOT_FIVE * jnp.sqrt(dist_sq)
    return (1.0 + scaled_dist + scaled_dist * scaled_dist / 3.0) * jnp.exp(-scaled_dist)


def split_groups(array, width):
    groups = array.shape[1] // width
    return array.reshape(array.shape[0], groups, width).transpose(1, 0, 2)


def tile_sums(row_groups, cols_x, cols_v, both):
    group_x, group_sq, group_v = row_groups
    cols_sq = jnp.sum(cols_x * cols_x, axis=0)
    start = jnp.zeros(cols_v.shape, jnp.float32)

    def one_group(carried, pieces):
        piece_x, piece_sq, piece_v = pieces
        kernel_tile = matern_tile(piece_x, piece_sq, cols_x, cols_sq)
        row_part = lax.dot_general(
            cols_v,
            kernel_tile,
            (((1,), (1,)), ((), ())),
            precision=lax.Precision.HIGHEST,
            preferred_element_type=jnp.float32,
        )
        if both:
            carried = carried + jnp.dot(
                piece_v,
                kernel_tile,
                precision=lax.Precision.HIGHEST,
                preferred_element_type=jnp.float32,
            )
        return (carried, row_part)

    col_part, row_parts = lax.scan(one_group, start, (group_x, group_sq, group_v))
    rows_total = row_parts.transpose(1, 0, 2).reshape(
        cols_v.shape[0], row_parts.shape[0] * row_parts.shape[2]
    )
    return (rows_total, col_part)


def on_device(features, vectors, lengthscales, noise_var, signal):
    scaled = features / lengthscales[:, None]
    width = vectors.shape[1]
    rows_x, rows_v = (
        lax.all_gather(scaled, "col", axis=1, tiled=True),
        lax.all_gather(vectors, "col", axis=1, tiled=True),
    )
    rows_sq = jnp.sum(rows_x * rows_x, axis=0)
    row_groups = (
        split_groups(rows_x, width),
        rows_sq.reshape(rows_sq.shape[0] // width, width),
        split_groups(rows_v, width),
    )
    half_loop = lax.axis_size("blk") // 2
    col_zeros = jnp.zeros(vectors.shape, jnp.float32)
    row_sums, unused = tile_sums(row_groups, scaled, vectors, False)

    def advance(index, carry):
        col_feat, col_vec, carried, totals = carry
        col_feat, col_vec, carried = shifted((col_feat, col_vec, carried), "blk", 1)
        row_part, col_part = tile_sums(row_groups, col_feat, col_vec, True)
        return (col_feat, col_vec, carried + col_part, totals + row_part)

    col_feat, col_vec, carried, row_sums = lax.fori_loop(
        1, half_loop, advance, (scaled, vectors, col_zeros, row_sums)
    )
    col_feat, col_vec = shifted((col_feat, col_vec), "blk", 1)
    last_rows, unused = tile_sums(row_groups, col_feat, col_vec, False)
    row_sums = row_sums + last_rows
    col_sums = shifted(carried, "blk", half_loop + 1)
    whole_rows = lax.psum(row_sums, "col")
    own_rows = lax.dynamic_slice_in_dim(whole_rows, lax.axis_index("col") * width, width, 1)
    return signal[0] * (own_rows + col_sums) + noise_var[None, :] * vectors


def solution(mesh):
    placed = (P(None, ("blk", "col")), P(None, ("blk", "col")), P(), P(("blk", "col")), P())
    return jax.shard_map(
        on_device, mesh=mesh, in_specs=placed, out_specs=P(None, ("blk", "col")), check_vma=False
    )
```

profile of v0, /device:TPU:1, one launch (start us, length us, event | category | flops | bytes accessed | tf_op | source)
XLA Modules:
  0.0 586.1 jit_solution(9279602517286392812)
XLA Ops:
  6.5 29.8 %all_gather.7 = f32[16,2048]{1,0:T(8,128)S(1)} all-gather(f32[16,128]{1,0:T(8,128)} %param.14), channel_id=1, replica_groups=mesh['blk'=32,'col'=16] {'col'}, dimensions={1}, use_global_device_ids=true | all-gather | bytes 139264 | tf_op jit(solution)/shard_map/all_gather | solution.py:69
  37.1 22.9 %all_gather.6 = f32[8,2048]{1,0:T(8,128)S(1)} all-gather(f32[8,128]{1,0:T(8,128)S(1)} %get-tuple-element.590), channel_id=1, replica_groups=mesh['blk'=32,'col'=16] {'col'}, dimensions={1}, use_global_device_ids=true | all-gather | bytes 69632 | tf_op jit(solution)/shard_map/all_gather | solution.py:68
  60.0 9.1 %while.51 = (s32[]{:T(128)}, f32[16,16,128]{2,1,0:T(8,128)S(1)}, f32[16,128]{1,0:T(8,128)S(1)}, f32[128]{0:T(128)S(1)}, f32[16,8,128]{2,1,0:T(8,128)S(1)}, /*ind...) while((s32[]{:T(128)}, f32[16,16,128]{2,1,0:T(8,128)S(1)}, f32[16,128]{1,0:T(8,128)S(1)}, ...), condition=%wide.region_3.4_spmd, body=%wide.region_2.3_spmd.sunk | while | flops 4898818 | bytes 157793 | solution.py:57
  69.3 360.3 %while.54 = (s32[]{:T(128)}, f32[8,128]{1,0:T(8,128)S(1)}, f32[16,128]{1,0:T(8,128)S(1)}, f32[16,128]{1,0:T(8,128)S(1)}, f32[16,2048]{1,0:T(8,128)S(1)}, /*index...) while((s32[]{:T(128)}, f32[8,128]{1,0:T(8,128)S(1)}, ...), condition=%wide.region_8.9_spmd.clone, body=%wide.region_4.8_spmd.clone.sunk | while | flops 8087430 | bytes 793566 | solution.py:87
  69.3 20.2 %collective-permute-start = (f32[8,128]{1,0:T(8,128)S(1)}, f32[8,128]{1,0:T(8,128)S(1)}, u32[]{:S(2)}, u32[]{:S(2)}) collective-permute-start(f32[8,128]{1,0:T(8,128)S(1)} %get-tuple-element.602), channel_id=1, source_target_pairs={{0,16},{16,32},{32,48},{48,64},{64,80},{80,96},{96,112},{112,128},... | collective-permute-start | bytes 12296 | tf_op jit(solution)/shard_map/while/body/eval_jaxpr/ppermute | solution.py:12
  89.5 1.9 collective-permute-start.1
  91.5 6.5 %collective-permute-start.2 = (f32[16,128]{1,0:T(8,128)S(1)}, f32[16,128]{1,0:T(8,128)S(1)}, u32[]{:S(2)}, u32[]{:S(2)}) collective-permute-start(f32[16,128]{1,0:T(8,128)S(1)} %broadcast_select_fusion.2), channel_id=1, source_target_pairs={{0,16},{16,32},{32,48},{48,64},{64,80},{80,96},{96,112},{112,128},... | collective-permute-start | bytes 24584 | tf_op jit(solution)/shard_map/while/body/eval_jaxpr/ppermute | solution.py:12
  98.0 12.0 %while.55 = (s32[]{:T(128)}, f32[16,128]{1,0:T(8,128)S(1)}, f32[16,16,128]{2,1,0:T(8,128)S(1)}, f32[16,16,128]{2,1,0:T(8,128)S(1)}, f32[16,128]{1,0:T(8,128)S(1)...) while((s32[]{:T(128)}, f32[16,128]{1,0:T(8,128)S(1)}, ...), condition=%wide.region_7.7_spmd.clone, body=%wide.region_6.6_spmd.clone.sunk | while | flops 8048643 | bytes 247943 | solution.py:57
  110.2 1.9 collective-permute-start
  112.1 4.4 collective-permute-start.1
  116.5 2.6 collective-permute-start.2
  119.1 12.0 %while.55 = (s32[]{:T(128)}, f32[16,128]{1,0:T(8,128)S(1)}, f32[16,16,128]{2,1,0:T(8,128)S(1)}, f32[16,16,128]{2,1,0:T(8,128)S(1)}, f32[16,128]{1,0:T(8,128)S(1)...) while((s32[]{:T(128)}, f32[16,128]{1,0:T(8,128)S(1)}, ...), condition=%wide.region_7.7_spmd.clone, body=%wide.region_6.6_spmd.clone.sunk | while | flops 8048643 | bytes 247943 | solution.py:57
  131.3 3.2 collective-permute-start
  134.5 1.9 collective-permute-start.1
  136.4 3.8 collective-permute-start.2
  140.3 12.0 %while.55 = (s32[]{:T(128)}, f32[16,128]{1,0:T(8,128)S(1)}, f32[16,16,128]{2,1,0:T(8,128)S(1)}, f32[16,16,128]{2,1,0:T(8,128)S(1)}, f32[16,128]{1,0:T(8,128)S(1)...) while((s32[]{:T(128)}, f32[16,128]{1,0:T(8,128)S(1)}, ...), condition=%wide.region_7.7_spmd.clone, body=%wide.region_6.6_spmd.clone.sunk | while | flops 8048643 | bytes 247943 | solution.py:57
  152.4 2.0 collective-permute-start
  154.4 4.0 collective-permute-start.1
  158.4 2.9 collective-permute-start.2
  161.7 12.0 %while.55 = (s32[]{:T(128)}, f32[16,128]{1,0:T(8,128)S(1)}, f32[16,16,128]{2,1,0:T(8,128)S(1)}, f32[16,16,128]{2,1,0:T(8,128)S(1)}, f32[16,128]{1,0:T(8,128)S(1)...) while((s32[]{:T(128)}, f32[16,128]{1,0:T(8,128)S(1)}, ...), condition=%wide.region_7.7_spmd.clone, body=%wide.region_6.6_spmd.clone.sunk | while | flops 8048643 | bytes 247943 | solution.py:57
  173.8 4.7 collective-permute-start
  178.5 1.9 collective-permute-start.1
  180.5 5.0 collective-permute-start.2
  185.6 12.0 %while.55 = (s32[]{:T(128)}, f32[16,128]{1,0:T(8,128)S(1)}, f32[16,16,128]{2,1,0:T(8,128)S(1)}, f32[16,16,128]{2,1,0:T(8,128)S(1)}, f32[16,128]{1,0:T(8,128)S(1)...) while((s32[]{:T(128)}, f32[16,128]{1,0:T(8,128)S(1)}, ...), condition=%wide.region_7.7_spmd.clone, body=%wide.region_6.6_spmd.clone.sunk | while | flops 8048643 | bytes 247943 | solution.py:57
  197.8 2.8 collective-permute-start
  200.6 1.9 collective-permute-start.1
  202.5 5.0 collective-permute-start.2
  208.2 12.0 %while.55 = (s32[]{:T(128)}, f32[16,128]{1,0:T(8,128)S(1)}, f32[16,16,128]{2,1,0:T(8,128)S(1)}, f32[16,16,128]{2,1,0:T(8,128)S(1)}, f32[16,128]{1,0:T(8,128)S(1)...) while((s32[]{:T(128)}, f32[16,128]{1,0:T(8,128)S(1)}, ...), condition=%wide.region_7.7_spmd.clone, body=%wide.region_6.6_spmd.clone.sunk | while | flops 8048643 | bytes 247943 | solution.py:57
  220.3 2.3 collective-permute-start
  222.6 1.9 collective-permute-start.1
  224.6 5.0 collective-permute-start.2
  231.4 12.0 %while.55 = (s32[]{:T(128)}, f32[16,128]{1,0:T(8,128)S(1)}, f32[16,16,128]{2,1,0:T(8,128)S(1)}, f32[16,16,128]{2,1,0:T(8,128)S(1)}, f32[16,128]{1,0:T(8,128)S(1)...) while((s32[]{:T(128)}, f32[16,128]{1,0:T(8,128)S(1)}, ...), condition=%wide.region_7.7_spmd.clone, body=%wide.region_6.6_spmd.clone.sunk | while | flops 8048643 | bytes 247943 | solution.py:57
  243.6 1.9 collective-permute-start
  245.5 1.9 collective-permute-start.1
  247.4 4.2 collective-permute-start.2
  254.7 12.0 %while.55 = (s32[]{:T(128)}, f32[16,128]{1,0:T(8,128)S(1)}, f32[16,16,128]{2,1,0:T(8,128)S(1)}, f32[16,16,128]{2,1,0:T(8,128)S(1)}, f32[16,128]{1,0:T(8,128)S(1)...) while((s32[]{:T(128)}, f32[16,128]{1,0:T(8,128)S(1)}, ...), condition=%wide.region_7.7_spmd.clone, body=%wide.region_6.6_spmd.clone.sunk | while | flops 8048643 | bytes 247943 | solution.py:57
  266.8 1.9 collective-permute-start
  268.7 1.9 collective-permute-start.1
  270.7 3.0 collective-permute-start.2
  273.7 2.3 collective-permute-done
  277.9 12.0 %while.55 = (s32[]{:T(128)}, f32[16,128]{1,0:T(8,128)S(1)}, f32[16,16,128]{2,1,0:T(8,128)S(1)}, f32[16,16,128]{2,1,0:T(8,128)S(1)}, f32[16,128]{1,0:T(8,128)S(1)...) while((s32[]{:T(128)}, f32[16,128]{1,0:T(8,128)S(1)}, ...), condition=%wide.region_7.7_spmd.clone, body=%wide.region_6.6_spmd.clone.sunk | while | flops 8048643 | bytes 247943 | solution.py:57
  290.1 1.9 collective-permute-start
  292.0 1.9 collective-permute-start.1
  293.9 1.9 collective-permute-start.2
  295.9 3.4 collective-permute-done
  301.2 12.0 %while.55 = (s32[]{:T(128)}, f32[16,128]{1,0:T(8,128)S(1)}, f32[16,16,128]{2,1,0:T(8,128)S(1)}, f32[16,16,128]{2,1,0:T(8,128)S(1)}, f32[16,128]{1,0:T(8,128)S(1)...) while((s32[]{:T(128)}, f32[16,128]{1,0:T(8,128)S(1)}, ...), condition=%wide.region_7.7_spmd.clone, body=%wide.region_6.6_spmd.clone.sunk | while | flops 8048643 | bytes 247943 | solution.py:57
  313.3 1.9 collective-permute-start
  319.1 3.4 collective-permute-done
  324.4 12.0 %while.55 = (s32[]{:T(128)}, f32[16,128]{1,0:T(8,128)S(1)}, f32[16,16,128]{2,1,0:T(8,128)S(1)}, f32[16,16,128]{2,1,0:T(8,128)S(1)}, f32[16,128]{1,0:T(8,128)S(1)...) while((s32[]{:T(128)}, f32[16,128]{1,0:T(8,128)S(1)}, ...), condition=%wide.region_7.7_spmd.clone, body=%wide.region_6.6_spmd.clone.sunk | while | flops 8048643 | bytes 247943 | solution.py:57
  342.4 3.4 collective-permute-done
  347.7 12.0 %while.55 = (s32[]{:T(128)}, f32[16,128]{1,0:T(8,128)S(1)}, f32[16,16,128]{2,1,0:T(8,128)S(1)}, f32[16,16,128]{2,1,0:T(8,128)S(1)}, f32[16,128]{1,0:T(8,128)S(1)...) while((s32[]{:T(128)}, f32[16,128]{1,0:T(8,128)S(1)}, ...), condition=%wide.region_7.7_spmd.clone, body=%wide.region_6.6_spmd.clone.sunk | while | flops 8048643 | bytes 247943 | solution.py:57
  359.8 1.9 collective-permute-start
  361.7 1.9 collective-permute-start.1
  363.7 1.9 collective-permute-start.2
  365.6 3.4 collective-permute-done
  370.9 12.0 %while.55 = (s32[]{:T(128)}, f32[16,128]{1,0:T(8,128)S(1)}, f32[16,16,128]{2,1,0:T(8,128)S(1)}, f32[16,16,128]{2,1,0:T(8,128)S(1)}, f32[16,128]{1,0:T(8,128)S(1)...) while((s32[]{:T(128)}, f32[16,128]{1,0:T(8,128)S(1)}, ...), condition=%wide.region_7.7_spmd.clone, body=%wide.region_6.6_spmd.clone.sunk | while | flops 8048643 | bytes 247943 | solution.py:57
  388.9 3.4 collective-permute-done
  394.2 12.0 %while.55 = (s32[]{:T(128)}, f32[16,128]{1,0:T(8,128)S(1)}, f32[16,16,128]{2,1,0:T(8,128)S(1)}, f32[16,16,128]{2,1,0:T(8,128)S(1)}, f32[16,128]{1,0:T(8,128)S(1)...) while((s32[]{:T(128)}, f32[16,128]{1,0:T(8,128)S(1)}, ...), condition=%wide.region_7.7_spmd.clone, body=%wide.region_6.6_spmd.clone.sunk | while | flops 8048643 | bytes 247943 | solution.py:57
  412.1 3.4 collective-permute-done
  417.4 12.0 %while.55 = (s32[]{:T(128)}, f32[16,128]{1,0:T(8,128)S(1)}, f32[16,16,128]{2,1,0:T(8,128)S(1)}, f32[16,16,128]{2,1,0:T(8,128)S(1)}, f32[16,128]{1,0:T(8,128)S(1)...) while((s32[]{:T(128)}, f32[16,128]{1,0:T(8,128)S(1)}, ...), condition=%wide.region_7.7_spmd.clone, body=%wide.region_6.6_spmd.clone.sunk | while | flops 8048643 | bytes 247943 | solution.py:57
  433.4 5.3 collective-permute-done.3
  440.7 9.1 %while.52 = (s32[]{:T(128)}, f32[16,16,128]{2,1,0:T(8,128)S(1)}, f32[16,128]{1,0:T(8,128)S(1)}, f32[128]{0:T(128)S(1)}, f32[16,8,128]{2,1,0:T(8,128)S(1)}, /*ind...) while((s32[]{:T(128)}, f32[16,16,128]{2,1,0:T(8,128)S(1)}, f32[16,128]{1,0:T(8,128)S(1)}, ...), condition=%wide.region_11.12_spmd, body=%wide.region_10.11_spmd.sunk | while | flops 4898818 | bytes 157793 | solution.py:57
  453.1 3.9 collective-permute-done.5
  456.9 121.0 %all-reduce.2.cloned.1.call-done = f32[16,2048]{1,0:T(8,128)} async-done(((f32[16,2048]{1,0:T(8,128)}), f32[16,2048]{1,0:T(8,128)}) %all-reduce.2.cloned.1.call-update) | async-done | bytes 131088 | tf_op jit(solution)/shard_map/psum | solution.py:94
  (1251 shorter events, 245.6 us)
Async XLA Ops:
  6.5 29.8 %copy-start = (f32[16,128]{1,0:T(8,128)S(1)}, f32[16,128]{1,0:T(8,128)}, u32[]{:S(2)}) copy-start(f32[16,128]{1,0:T(8,128)} %param.14) | copy-start | bytes 24580
  6.5 571.4 %all-reduce.2.cloned.1.call-start = ((), (), s32[]{:S(2)}) async-start(), calls=%async_computation | async-start | bytes 262144 | tf_op jit(solution)/shard_map/psum | solution.py:94
  36.3 0.7 copy-start.1
  36.3 0.7 copy-start.3
  69.3 28.7 %collective-permute-start = (f32[8,128]{1,0:T(8,128)S(1)}, f32[8,128]{1,0:T(8,128)S(1)}, u32[]{:S(2)}, u32[]{:S(2)}) collective-permute-start(f32[8,128]{1,0:T(8,128)S(1)} %get-tuple-element.602), channel_id=1, source_target_pairs={{0,16},{16,32},{32,48},{48,64},{64,80},{80,96},{96,112},{112,128},... | collective-permute-start | bytes 12296 | tf_op jit(solution)/shard_map/while/body/eval_jaxpr/ppermute | solution.py:12
  89.5 8.5 %collective-permute-start.1 = (f32[16,128]{1,0:T(8,128)S(1)}, f32[16,128]{1,0:T(8,128)S(1)}, u32[]{:S(2)}, u32[]{:S(2)}) collective-permute-start(f32[16,128]{1,0:T(8,128)S(1)} %get-tuple-element.603), channel_id=1, source_target_pairs={{0,16},{16,32},{32,48},{48,64},{64,80},{80,96},{96,112},{112,128},... | collective-permute-start | bytes 24584 | tf_op jit(solution)/shard_map/while/body/eval_jaxpr/ppermute | solution.py:12
  91.5 18.7 %collective-permute-start.2 = (f32[16,128]{1,0:T(8,128)S(1)}, f32[16,128]{1,0:T(8,128)S(1)}, u32[]{:S(2)}, u32[]{:S(2)}) collective-permute-start(f32[16,128]{1,0:T(8,128)S(1)} %broadcast_select_fusion.2), channel_id=1, source_target_pairs={{0,16},{16,32},{32,48},{48,64},{64,80},{80,96},{96,112},{112,128},... | collective-permute-start | bytes 24584 | tf_op jit(solution)/shard_map/while/body/eval_jaxpr/ppermute | solution.py:12
  110.2 8.9 %collective-permute-start = (f32[8,128]{1,0:T(8,128)S(1)}, f32[8,128]{1,0:T(8,128)S(1)}, u32[]{:S(2)}, u32[]{:S(2)}) collective-permute-start(f32[8,128]{1,0:T(8,128)S(1)} %get-tuple-element.602), channel_id=1, source_target_pairs={{0,16},{16,32},{32,48},{48,64},{64,80},{80,96},{96,112},{112,128},... | collective-permute-start | bytes 12296 | tf_op jit(solution)/shard_map/while/body/eval_jaxpr/ppermute | solution.py:12
  112.1 7.0 %collective-permute-start.1 = (f32[16,128]{1,0:T(8,128)S(1)}, f32[16,128]{1,0:T(8,128)S(1)}, u32[]{:S(2)}, u32[]{:S(2)}) collective-permute-start(f32[16,128]{1,0:T(8,128)S(1)} %get-tuple-element.603), channel_id=1, source_target_pairs={{0,16},{16,32},{32,48},{48,64},{64,80},{80,96},{96,112},{112,128},... | collective-permute-start | bytes 24584 | tf_op jit(solution)/shard_map/while/body/eval_jaxpr/ppermute | solution.py:12
  116.5 14.8 %collective-permute-start.2 = (f32[16,128]{1,0:T(8,128)S(1)}, f32[16,128]{1,0:T(8,128)S(1)}, u32[]{:S(2)}, u32[]{:S(2)}) collective-permute-start(f32[16,128]{1,0:T(8,128)S(1)} %broadcast_select_fusion.2), channel_id=1, source_target_pairs={{0,16},{16,32},{32,48},{48,64},{64,80},{80,96},{96,112},{112,128},... | collective-permute-start | bytes 24584 | tf_op jit(solution)/shard_map/while/body/eval_jaxpr/ppermute | solution.py:12
  131.3 8.9 %collective-permute-start = (f32[8,128]{1,0:T(8,128)S(1)}, f32[8,128]{1,0:T(8,128)S(1)}, u32[]{:S(2)}, u32[]{:S(2)}) collective-permute-start(f32[8,128]{1,0:T(8,128)S(1)} %get-tuple-element.602), channel_id=1, source_target_pairs={{0,16},{16,32},{32,48},{48,64},{64,80},{80,96},{96,112},{112,128},... | collective-permute-start | bytes 12296 | tf_op jit(solution)/shard_map/while/body/eval_jaxpr/ppermute | solution.py:12
  134.5 5.8 collective-permute-start.1
  136.4 16.0 %collective-permute-start.2 = (f32[16,128]{1,0:T(8,128)S(1)}, f32[16,128]{1,0:T(8,128)S(1)}, u32[]{:S(2)}, u32[]{:S(2)}) collective-permute-start(f32[16,128]{1,0:T(8,128)S(1)} %broadcast_select_fusion.2), channel_id=1, source_target_pairs={{0,16},{16,32},{32,48},{48,64},{64,80},{80,96},{96,112},{112,128},... | collective-permute-start | bytes 24584 | tf_op jit(solution)/shard_map/while/body/eval_jaxpr/ppermute | solution.py:12
  152.4 8.9 %collective-permute-start = (f32[8,128]{1,0:T(8,128)S(1)}, f32[8,128]{1,0:T(8,128)S(1)}, u32[]{:S(2)}, u32[]{:S(2)}) collective-permute-start(f32[8,128]{1,0:T(8,128)S(1)} %get-tuple-element.602), channel_id=1, source_target_pairs={{0,16},{16,32},{32,48},{48,64},{64,80},{80,96},{96,112},{112,128},... | collective-permute-start | bytes 12296 | tf_op jit(solution)/shard_map/while/body/eval_jaxpr/ppermute | solution.py:12
  154.4 7.2 %collective-permute-start.1 = (f32[16,128]{1,0:T(8,128)S(1)}, f32[16,128]{1,0:T(8,128)S(1)}, u32[]{:S(2)}, u32[]{:S(2)}) collective-permute-start(f32[16,128]{1,0:T(8,128)S(1)} %get-tuple-element.603), channel_id=1, source_target_pairs={{0,16},{16,32},{32,48},{48,64},{64,80},{80,96},{96,112},{112,128},... | collective-permute-start | bytes 24584 | tf_op jit(solution)/shard_map/while/body/eval_jaxpr/ppermute | solution.py:12
  158.4 15.3 %collective-permute-start.2 = (f32[16,128]{1,0:T(8,128)S(1)}, f32[16,128]{1,0:T(8,128)S(1)}, u32[]{:S(2)}, u32[]{:S(2)}) collective-permute-start(f32[16,128]{1,0:T(8,128)S(1)} %broadcast_select_fusion.2), channel_id=1, source_target_pairs={{0,16},{16,32},{32,48},{48,64},{64,80},{80,96},{96,112},{112,128},... | collective-permute-start | bytes 24584 | tf_op jit(solution)/shard_map/while/body/eval_jaxpr/ppermute | solution.py:12
  173.8 11.7 %collective-permute-start = (f32[8,128]{1,0:T(8,128)S(1)}, f32[8,128]{1,0:T(8,128)S(1)}, u32[]{:S(2)}, u32[]{:S(2)}) collective-permute-start(f32[8,128]{1,0:T(8,128)S(1)} %get-tuple-element.602), channel_id=1, source_target_pairs={{0,16},{16,32},{32,48},{48,64},{64,80},{80,96},{96,112},{112,128},... | collective-permute-start | bytes 12296 | tf_op jit(solution)/shard_map/while/body/eval_jaxpr/ppermute | solution.py:12
  178.5 7.0 %collective-permute-start.1 = (f32[16,128]{1,0:T(8,128)S(1)}, f32[16,128]{1,0:T(8,128)S(1)}, u32[]{:S(2)}, u32[]{:S(2)}) collective-permute-start(f32[16,128]{1,0:T(8,128)S(1)} %get-tuple-element.603), channel_id=1, source_target_pairs={{0,16},{16,32},{32,48},{48,64},{64,80},{80,96},{96,112},{112,128},... | collective-permute-start | bytes 24584 | tf_op jit(solution)/shard_map/while/body/eval_jaxpr/ppermute | solution.py:12
  180.5 17.2 %collective-permute-start.2 = (f32[16,128]{1,0:T(8,128)S(1)}, f32[16,128]{1,0:T(8,128)S(1)}, u32[]{:S(2)}, u32[]{:S(2)}) collective-permute-start(f32[16,128]{1,0:T(8,128)S(1)} %broadcast_select_fusion.2), channel_id=1, source_target_pairs={{0,16},{16,32},{32,48},{48,64},{64,80},{80,96},{96,112},{112,128},... | collective-permute-start | bytes 24584 | tf_op jit(solution)/shard_map/while/body/eval_jaxpr/ppermute | solution.py:12
  197.8 9.8 %collective-permute-start = (f32[8,128]{1,0:T(8,128)S(1)}, f32[8,128]{1,0:T(8,128)S(1)}, u32[]{:S(2)}, u32[]{:S(2)}) collective-permute-start(f32[8,128]{1,0:T(8,128)S(1)} %get-tuple-element.602), channel_id=1, source_target_pairs={{0,16},{16,32},{32,48},{48,64},{64,80},{80,96},{96,112},{112,128},... | collective-permute-start | bytes 12296 | tf_op jit(solution)/shard_map/while/body/eval_jaxpr/ppermute | solution.py:12
  200.6 7.6 %collective-permute-start.1 = (f32[16,128]{1,0:T(8,128)S(1)}, f32[16,128]{1,0:T(8,128)S(1)}, u32[]{:S(2)}, u32[]{:S(2)}) collective-permute-start(f32[16,128]{1,0:T(8,128)S(1)} %get-tuple-element.603), channel_id=1, source_target_pairs={{0,16},{16,32},{32,48},{48,64},{64,80},{80,96},{96,112},{112,128},... | collective-permute-start | bytes 24584 | tf_op jit(solution)/shard_map/while/body/eval_jaxpr/ppermute | solution.py:12
  202.5 17.7 %collective-permute-start.2 = (f32[16,128]{1,0:T(8,128)S(1)}, f32[16,128]{1,0:T(8,128)S(1)}, u32[]{:S(2)}, u32[]{:S(2)}) collective-permute-start(f32[16,128]{1,0:T(8,128)S(1)} %broadcast_select_fusion.2), channel_id=1, source_target_pairs={{0,16},{16,32},{32,48},{48,64},{64,80},{80,96},{96,112},{112,128},... | collective-permute-start | bytes 24584 | tf_op jit(solution)/shard_map/while/body/eval_jaxpr/ppermute | solution.py:12
  220.3 9.3 %collective-permute-start = (f32[8,128]{1,0:T(8,128)S(1)}, f32[8,128]{1,0:T(8,128)S(1)}, u32[]{:S(2)}, u32[]{:S(2)}) collective-permute-start(f32[8,128]{1,0:T(8,128)S(1)} %get-tuple-element.602), channel_id=1, source_target_pairs={{0,16},{16,32},{32,48},{48,64},{64,80},{80,96},{96,112},{112,128},... | collective-permute-start | bytes 12296 | tf_op jit(solution)/shard_map/while/body/eval_jaxpr/ppermute | solution.py:12
  222.6 8.8 %collective-permute-start.1 = (f32[16,128]{1,0:T(8,128)S(1)}, f32[16,128]{1,0:T(8,128)S(1)}, u32[]{:S(2)}, u32[]{:S(2)}) collective-permute-start(f32[16,128]{1,0:T(8,128)S(1)} %get-tuple-element.603), channel_id=1, source_target_pairs={{0,16},{16,32},{32,48},{48,64},{64,80},{80,96},{96,112},{112,128},... | collective-permute-start | bytes 24584 | tf_op jit(solution)/shard_map/while/body/eval_jaxpr/ppermute | solution.py:12
  224.6 18.9 %collective-permute-start.2 = (f32[16,128]{1,0:T(8,128)S(1)}, f32[16,128]{1,0:T(8,128)S(1)}, u32[]{:S(2)}, u32[]{:S(2)}) collective-permute-start(f32[16,128]{1,0:T(8,128)S(1)} %broadcast_select_fusion.2), channel_id=1, source_target_pairs={{0,16},{16,32},{32,48},{48,64},{64,80},{80,96},{96,112},{112,128},... | collective-permute-start | bytes 24584 | tf_op jit(solution)/shard_map/while/body/eval_jaxpr/ppermute | solution.py:12
  243.6 9.2 %collective-permute-start = (f32[8,128]{1,0:T(8,128)S(1)}, f32[8,128]{1,0:T(8,128)S(1)}, u32[]{:S(2)}, u32[]{:S(2)}) collective-permute-start(f32[8,128]{1,0:T(8,128)S(1)} %get-tuple-element.602), channel_id=1, source_target_pairs={{0,16},{16,32},{32,48},{48,64},{64,80},{80,96},{96,112},{112,128},... | collective-permute-start | bytes 12296 | tf_op jit(solution)/shard_map/while/body/eval_jaxpr/ppermute | solution.py:12
  245.5 9.2 %collective-permute-start.1 = (f32[16,128]{1,0:T(8,128)S(1)}, f32[16,128]{1,0:T(8,128)S(1)}, u32[]{:S(2)}, u32[]{:S(2)}) collective-permute-start(f32[16,128]{1,0:T(8,128)S(1)} %get-tuple-element.603), channel_id=1, source_target_pairs={{0,16},{16,32},{32,48},{48,64},{64,80},{80,96},{96,112},{112,128},... | collective-permute-start | bytes 24584 | tf_op jit(solution)/shard_map/while/body/eval_jaxpr/ppermute | solution.py:12
  247.4 19.3 %collective-permute-start.2 = (f32[16,128]{1,0:T(8,128)S(1)}, f32[16,128]{1,0:T(8,128)S(1)}, u32[]{:S(2)}, u32[]{:S(2)}) collective-permute-start(f32[16,128]{1,0:T(8,128)S(1)} %broadcast_select_fusion.2), channel_id=1, source_target_pairs={{0,16},{16,32},{32,48},{48,64},{64,80},{80,96},{96,112},{112,128},... | collective-permute-start | bytes 24584 | tf_op jit(solution)/shard_map/while/body/eval_jaxpr/ppermute | solution.py:12
  266.8 9.2 %collective-permute-start = (f32[8,128]{1,0:T(8,128)S(1)}, f32[8,128]{1,0:T(8,128)S(1)}, u32[]{:S(2)}, u32[]{:S(2)}) collective-permute-start(f32[8,128]{1,0:T(8,128)S(1)} %get-tuple-element.602), channel_id=1, source_target_pairs={{0,16},{16,32},{32,48},{48,64},{64,80},{80,96},{96,112},{112,128},... | collective-permute-start | bytes 12296 | tf_op jit(solution)/shard_map/while/body/eval_jaxpr/ppermute | solution.py:12
  268.7 9.2 %collective-permute-start.1 = (f32[16,128]{1,0:T(8,128)S(1)}, f32[16,128]{1,0:T(8,128)S(1)}, u32[]{:S(2)}, u32[]{:S(2)}) collective-permute-start(f32[16,128]{1,0:T(8,128)S(1)} %get-tuple-element.603), channel_id=1, source_target_pairs={{0,16},{16,32},{32,48},{48,64},{64,80},{80,96},{96,112},{112,128},... | collective-permute-start | bytes 24584 | tf_op jit(solution)/shard_map/while/body/eval_jaxpr/ppermute | solution.py:12
  270.7 19.3 %collective-permute-start.2 = (f32[16,128]{1,0:T(8,128)S(1)}, f32[16,128]{1,0:T(8,128)S(1)}, u32[]{:S(2)}, u32[]{:S(2)}) collective-permute-start(f32[16,128]{1,0:T(8,128)S(1)} %broadcast_select_fusion.2), channel_id=1, source_target_pairs={{0,16},{16,32},{32,48},{48,64},{64,80},{80,96},{96,112},{112,128},... | collective-permute-start | bytes 24584 | tf_op jit(solution)/shard_map/while/body/eval_jaxpr/ppermute | solution.py:12
  290.1 9.2 %collective-permute-start = (f32[8,128]{1,0:T(8,128)S(1)}, f32[8,128]{1,0:T(8,128)S(1)}, u32[]{:S(2)}, u32[]{:S(2)}) collective-permute-start(f32[8,128]{1,0:T(8,128)S(1)} %get-tuple-element.602), channel_id=1, source_target_pairs={{0,16},{16,32},{32,48},{48,64},{64,80},{80,96},{96,112},{112,128},... | collective-permute-start | bytes 12296 | tf_op jit(solution)/shard_map/while/body/eval_jaxpr/ppermute | solution.py:12
  292.0 9.2 %collective-permute-start.1 = (f32[16,128]{1,0:T(8,128)S(1)}, f32[16,128]{1,0:T(8,128)S(1)}, u32[]{:S(2)}, u32[]{:S(2)}) collective-permute-start(f32[16,128]{1,0:T(8,128)S(1)} %get-tuple-element.603), channel_id=1, source_target_pairs={{0,16},{16,32},{32,48},{48,64},{64,80},{80,96},{96,112},{112,128},... | collective-permute-start | bytes 24584 | tf_op jit(solution)/shard_map/while/body/eval_jaxpr/ppermute | solution.py:12
  293.9 19.3 %collective-permute-start.2 = (f32[16,128]{1,0:T(8,128)S(1)}, f32[16,128]{1,0:T(8,128)S(1)}, u32[]{:S(2)}, u32[]{:S(2)}) collective-permute-start(f32[16,128]{1,0:T(8,128)S(1)} %broadcast_select_fusion.2), channel_id=1, source_target_pairs={{0,16},{16,32},{32,48},{48,64},{64,80},{80,96},{96,112},{112,128},... | collective-permute-start | bytes 24584 | tf_op jit(solution)/shard_map/while/body/eval_jaxpr/ppermute | solution.py:12
  313.3 9.2 %collective-permute-start = (f32[8,128]{1,0:T(8,128)S(1)}, f32[8,128]{1,0:T(8,128)S(1)}, u32[]{:S(2)}, u32[]{:S(2)}) collective-permute-start(f32[8,128]{1,0:T(8,128)S(1)} %get-tuple-element.602), channel_id=1, source_target_pairs={{0,16},{16,32},{32,48},{48,64},{64,80},{80,96},{96,112},{112,128},... | collective-permute-start | bytes 12296 | tf_op jit(solution)/shard_map/while/body/eval_jaxpr/ppermute | solution.py:12
  315.2 9.2 %collective-permute-start.1 = (f32[16,128]{1,0:T(8,128)S(1)}, f32[16,128]{1,0:T(8,128)S(1)}, u32[]{:S(2)}, u32[]{:S(2)}) collective-permute-start(f32[16,128]{1,0:T(8,128)S(1)} %get-tuple-element.603), channel_id=1, source_target_pairs={{0,16},{16,32},{32,48},{48,64},{64,80},{80,96},{96,112},{112,128},... | collective-permute-start | bytes 24584 | tf_op jit(solution)/shard_map/while/body/eval_jaxpr/ppermute | solution.py:12
  317.2 19.3 %collective-permute-start.2 = (f32[16,128]{1,0:T(8,128)S(1)}, f32[16,128]{1,0:T(8,128)S(1)}, u32[]{:S(2)}, u32[]{:S(2)}) collective-permute-start(f32[16,128]{1,0:T(8,128)S(1)} %broadcast_select_fusion.2), channel_id=1, source_target_pairs={{0,16},{16,32},{32,48},{48,64},{64,80},{80,96},{96,112},{112,128},... | collective-permute-start | bytes 24584 | tf_op jit(solution)/shard_map/while/body/eval_jaxpr/ppermute | solution.py:12
  336.6 9.2 %collective-permute-start = (f32[8,128]{1,0:T(8,128)S(1)}, f32[8,128]{1,0:T(8,128)S(1)}, u32[]{:S(2)}, u32[]{:S(2)}) collective-permute-start(f32[8,128]{1,0:T(8,128)S(1)} %get-tuple-element.602), channel_id=1, source_target_pairs={{0,16},{16,32},{32,48},{48,64},{64,80},{80,96},{96,112},{112,128},... | collective-permute-start | bytes 12296 | tf_op jit(solution)/shard_map/while/body/eval_jaxpr/ppermute | solution.py:12
  338.5 9.2 %collective-permute-start.1 = (f32[16,128]{1,0:T(8,128)S(1)}, f32[16,128]{1,0:T(8,128)S(1)}, u32[]{:S(2)}, u32[]{:S(2)}) collective-permute-start(f32[16,128]{1,0:T(8,128)S(1)} %get-tuple-element.603), channel_id=1, source_target_pairs={{0,16},{16,32},{32,48},{48,64},{64,80},{80,96},{96,112},{112,128},... | collective-permute-start | bytes 24584 | tf_op jit(solution)/shard_map/while/body/eval_jaxpr/ppermute | solution.py:12
  340.4 19.3 %collective-permute-start.2 = (f32[16,128]{1,0:T(8,128)S(1)}, f32[16,128]{1,0:T(8,128)S(1)}, u32[]{:S(2)}, u32[]{:S(2)}) collective-permute-start(f32[16,128]{1,0:T(8,128)S(1)} %broadcast_select_fusion.2), channel_id=1, source_target_pairs={{0,16},{16,32},{32,48},{48,64},{64,80},{80,96},{96,112},{112,128},... | collective-permute-start | bytes 24584 | tf_op jit(solution)/shard_map/while/body/eval_jaxpr/ppermute | solution.py:12
  359.8 9.2 %collective-permute-start = (f32[8,128]{1,0:T(8,128)S(1)}, f32[8,128]{1,0:T(8,128)S(1)}, u32[]{:S(2)}, u32[]{:S(2)}) collective-permute-start(f32[8,128]{1,0:T(8,128)S(1)} %get-tuple-element.602), channel_id=1, source_target_pairs={{0,16},{16,32},{32,48},{48,64},{64,80},{80,96},{96,112},{112,128},... | collective-permute-start | bytes 12296 | tf_op jit(solution)/shard_map/while/body/eval_jaxpr/ppermute | solution.py:12
  361.7 9.2 %collective-permute-start.1 = (f32[16,128]{1,0:T(8,128)S(1)}, f32[16,128]{1,0:T(8,128)S(1)}, u32[]{:S(2)}, u32[]{:S(2)}) collective-permute-start(f32[16,128]{1,0:T(8,128)S(1)} %get-tuple-element.603), channel_id=1, source_target_pairs={{0,16},{16,32},{32,48},{48,64},{64,80},{80,96},{96,112},{112,128},... | collective-permute-start | bytes 24584 | tf_op jit(solution)/shard_map/while/body/eval_jaxpr/ppermute | solution.py:12
  363.7 19.3 %collective-permute-start.2 = (f32[16,128]{1,0:T(8,128)S(1)}, f32[16,128]{1,0:T(8,128)S(1)}, u32[]{:S(2)}, u32[]{:S(2)}) collective-permute-start(f32[16,128]{1,0:T(8,128)S(1)} %broadcast_select_fusion.2), channel_id=1, source_target_pairs={{0,16},{16,32},{32,48},{48,64},{64,80},{80,96},{96,112},{112,128},... | collective-permute-start | bytes 24584 | tf_op jit(solution)/shard_map/while/body/eval_jaxpr/ppermute | solution.py:12
  383.1 9.2 %collective-permute-start = (f32[8,128]{1,0:T(8,128)S(1)}, f32[8,128]{1,0:T(8,128)S(1)}, u32[]{:S(2)}, u32[]{:S(2)}) collective-permute-start(f32[8,128]{1,0:T(8,128)S(1)} %get-tuple-element.602), channel_id=1, source_target_pairs={{0,16},{16,32},{32,48},{48,64},{64,80},{80,96},{96,112},{112,128},... | collective-permute-start | bytes 12296 | tf_op jit(solution)/shard_map/while/body/eval_jaxpr/ppermute | solution.py:12
  385.0 9.2 %collective-permute-start.1 = (f32[16,128]{1,0:T(8,128)S(1)}, f32[16,128]{1,0:T(8,128)S(1)}, u32[]{:S(2)}, u32[]{:S(2)}) collective-permute-start(f32[16,128]{1,0:T(8,128)S(1)} %get-tuple-element.603), channel_id=1, source_target_pairs={{0,16},{16,32},{32,48},{48,64},{64,80},{80,96},{96,112},{112,128},... | collective-permute-start | bytes 24584 | tf_op jit(solution)/shard_map/while/body/eval_jaxpr/ppermute | solution.py:12
  386.9 19.3 %collective-permute-start.2 = (f32[16,128]{1,0:T(8,128)S(1)}, f32[16,128]{1,0:T(8,128)S(1)}, u32[]{:S(2)}, u32[]{:S(2)}) collective-permute-start(f32[16,128]{1,0:T(8,128)S(1)} %broadcast_select_fusion.2), channel_id=1, source_target_pairs={{0,16},{16,32},{32,48},{48,64},{64,80},{80,96},{96,112},{112,128},... | collective-permute-start | bytes 24584 | tf_op jit(solution)/shard_map/while/body/eval_jaxpr/ppermute | solution.py:12
  406.3 9.2 %collective-permute-start = (f32[8,128]{1,0:T(8,128)S(1)}, f32[8,128]{1,0:T(8,128)S(1)}, u32[]{:S(2)}, u32[]{:S(2)}) collective-permute-start(f32[8,128]{1,0:T(8,128)S(1)} %get-tuple-element.602), channel_id=1, source_target_pairs={{0,16},{16,32},{32,48},{48,64},{64,80},{80,96},{96,112},{112,128},... | collective-permute-start | bytes 12296 | tf_op jit(solution)/shard_map/while/body/eval_jaxpr/ppermute | solution.py:12
  408.2 9.2 %collective-permute-start.1 = (f32[16,128]{1,0:T(8,128)S(1)}, f32[16,128]{1,0:T(8,128)S(1)}, u32[]{:S(2)}, u32[]{:S(2)}) collective-permute-start(f32[16,128]{1,0:T(8,128)S(1)} %get-tuple-element.603), channel_id=1, source_target_pairs={{0,16},{16,32},{32,48},{48,64},{64,80},{80,96},{96,112},{112,128},... | collective-permute-start | bytes 24584 | tf_op jit(solution)/shard_map/while/body/eval_jaxpr/ppermute | solution.py:12
  410.2 19.3 %collective-permute-start.2 = (f32[16,128]{1,0:T(8,128)S(1)}, f32[16,128]{1,0:T(8,128)S(1)}, u32[]{:S(2)}, u32[]{:S(2)}) collective-permute-start(f32[16,128]{1,0:T(8,128)S(1)} %broadcast_select_fusion.2), channel_id=1, source_target_pairs={{0,16},{16,32},{32,48},{48,64},{64,80},{80,96},{96,112},{112,128},... | collective-permute-start | bytes 24584 | tf_op jit(solution)/shard_map/while/body/eval_jaxpr/ppermute | solution.py:12
  429.6 9.2 %collective-permute-start.3 = (f32[8,128]{1,0:T(8,128)S(1)}, f32[8,128]{1,0:T(8,128)S(1)}, u32[]{:S(2)}, u32[]{:S(2)}) collective-permute-start(f32[8,128]{1,0:T(8,128)S(1)} %get-tuple-element.174), channel_id=1, source_target_pairs={{0,16},{16,32},{32,48},{48,64},{64,80},{80,96},{96,112},{112,128},... | collective-permute-start | bytes 12296 | tf_op jit(solution)/shard_map/ppermute | solution.py:12
  431.5 9.2 %collective-permute-start.4 = (f32[16,128]{1,0:T(8,128)S(1)}, f32[16,128]{1,0:T(8,128)S(1)}, u32[]{:S(2)}, u32[]{:S(2)}) collective-permute-start(f32[16,128]{1,0:T(8,128)S(1)} %get-tuple-element.175), channel_id=1, source_target_pairs={{0,16},{16,32},{32,48},{48,64},{64,80},{80,96},{96,112},{112,128},... | collective-permute-start | bytes 24584 | tf_op jit(solution)/shard_map/ppermute | solution.py:12
  450.5 6.5 %collective-permute-start.5 = (f32[16,128]{1,0:T(8,128)S(1)}, f32[16,128]{1,0:T(8,128)S(1)}, u32[]{:S(2)}, u32[]{:S(2)}) collective-permute-start(f32[16,128]{1,0:T(8,128)S(1)} %get-tuple-element.177), channel_id=1, source_target_pairs={{0,272},{16,288},{32,304},{48,320},{64,336},{80,352},{96,368},{112... | collective-permute-start | bytes 24584 | tf_op jit(solution)/shard_map/ppermute | solution.py:12
  453.1 124.9 %copy-start.2 = (f32[128]{0:T(128)S(1)}, f32[128]{0:T(128)}, u32[]{:S(2)}) copy-start(f32[128]{0:T(128)} %param.16) | copy-start | bytes 1540
Sparse Core Ops, SparseCore 0:
  450.6 127.3 all-reduce.1
where the time goes:
time: 598 us; the launch traced here: 586 us
  matrix products  181 us (30%)
  waiting for transfers between devices  174 us (29%)
  starting transfers between devices  141 us (24%)
  blocking collectives  52.7 us (9%)
  between operations  14.1 us (2%)
  local copies, waits for them, and re-layouts  13.5 us (2%)
  loops' own time  6.67 us (1%)
    ppermute x48, starting transfers between devices, shifted(): return lax.ppermute(value, axis, pairs)  141 us
    psum x1, waiting for transfers between devices, on_device(): whole_rows = lax.psum(row_sums, 'col')  121 us
    dot_general x272, matrix products, matern_tile(): lax.dot_general(rows_x, cols_x, (((0,), (0,)), ((), ())), precision=lax.P...  91.2 us
    ppermute x48, waiting for transfers between devices, shifted(): return lax.ppermute(value, axis, pairs)  52.5 us
    dot_general x272, matrix products, one_group(): lax.dot_general(cols_v, kernel_tile, (((1,), (1,)), ((), ())), precision=...  52.4 us
    dot_general x240, matrix products, one_group(): jnp.dot(piece_v, kernel_tile, precision=lax.Precision.HIGHEST, preferred_...  37 us
    all_gather x1, blocking collectives, on_device(): lax.all_gather(vectors, 'col', axis=1, tiled=True)  29.8 us
    all_gather x1, blocking collectives, on_device(): lax.all_gather(scaled, 'col', axis=1, tiled=True)  22.9 us
  transfers between devices with their start and end apart: 49, of which 23 were waited for; matrix products, arithmetic and copies ran while one was open for 30% of the time, Pallas kernels for 0%

commit v1 on v0

v1 whole, which is shorter than its diff:
```python
import functools
import math

import jax
import jax.numpy as jnp
from jax import lax
from jax.experimental import pallas as pl
from jax.experimental.pallas import tpu as pltpu
from jax.sharding import PartitionSpec as P

MESH = pl.DeviceIdType.MESH
F32 = jnp.float32
BF16 = jnp.bfloat16
SCALE = math.sqrt(5.0 / 3.0)
HALF3 = math.sqrt(3.0) / 2.0
RATE = -math.sqrt(3.0) * math.log2(math.e)
TINY = 1e-30
WIDTH = 128
FEAT = 8
PROBES = 16
DEPTH = 64


def split3(value):
    high = value.astype(BF16).astype(F32)
    rest = value - high
    mid = rest.astype(BF16).astype(F32)
    return high, mid, rest - mid


def norms3(points):
    return split3(jnp.sum(points * points, axis=0, keepdims=True))


def row_side(points):
    high, mid, low = split3(points)
    nh, nm, nl = norms3(points)
    one, zero = jnp.ones_like(nh), jnp.zeros_like(nh)
    extra = jnp.concatenate([nh, nm, nl, one, one, one, zero, zero], axis=0)
    pad = jnp.zeros_like(points)
    return jnp.concatenate([high, high, mid, mid, high, low, extra, pad], axis=0)


def col_side(points):
    high, mid, low = (-2.0 * part for part in split3(points))
    nh, nm, nl = norms3(points)
    one, zero = jnp.ones_like(nh), jnp.zeros_like(nh)
    extra = jnp.concatenate([one, one, one, nh, nm, nl, zero, zero], axis=0)
    pad = jnp.zeros_like(points)
    return jnp.concatenate([high, mid, high, mid, low, high, extra, pad], axis=0)


def matern(dist_sq):
    floor = jnp.maximum(dist_sq, TINY)
    dist = floor * lax.rsqrt(floor)
    decay = jnp.exp2(dist * RATE)
    shifted = dist + HALF3
    return (shifted * shifted + 0.25) * decay


def tile_sums(cols_t, vecs, rows):
    kernel_tile = matern(jnp.dot(cols_t, rows, preferred_element_type=F32))
    high = kernel_tile.astype(BF16)
    low = (kernel_tile - high.astype(F32)).astype(BF16)
    both = jnp.dot(vecs, high, preferred_element_type=F32)
    return both[:PROBES] + both[PROBES:] + jnp.dot(vecs[:PROBES], low, preferred_element_type=F32)


def kernel(nb, nc, ls_ref, feat_ref, vec_ref, out_ref, mine, colbuf, rowbuf, rows, cols_t, vecs, acc, parts,
           row_send, row_recv, col_send, col_recv, part_send, part_recv):
    blk, col = lax.axis_index("blk"), lax.axis_index("col")

    def row_peer(step):
        return (blk, lax.rem(col + step, nc))

    def col_peer(step):
        return (lax.rem(blk + step, nb), col)

    barrier = pltpu.get_barrier_semaphore()

    def greet(peer):
        def body(step, carry):
            pl.semaphore_signal(barrier, inc=1, device_id=peer(step), device_id_type=MESH)
            return carry
        return body

    lax.fori_loop(1, nc, greet(row_peer), 0)
    lax.fori_loop(1, nb, greet(col_peer), 0)

    feature = lax.broadcasted_iota(jnp.int32, (FEAT, WIDTH), 0)
    lengths = jnp.full((FEAT, WIDTH), ls_ref[0], F32)
    for k in range(1, FEAT):
        lengths = jnp.where(feature == k, ls_ref[k], lengths)
    mine[:FEAT] = feat_ref[...] / lengths * SCALE
    mine[FEAT:] = vec_ref[...]
    acc[...] = jnp.zeros_like(acc)
    pl.semaphore_wait(barrier, nb + nc - 2)

    def row_copy(step):
        return pltpu.make_async_remote_copy(
            src_ref=mine.at[:FEAT], dst_ref=rowbuf.at[step], send_sem=row_send.at[step], recv_sem=row_recv.at[step],
            device_id=row_peer(step), device_id_type=MESH)

    def col_copy(step):
        return pltpu.make_async_remote_copy(
            src_ref=mine, dst_ref=colbuf.at[step], send_sem=col_send.at[step], recv_sem=col_recv.at[step],
            device_id=col_peer(step), device_id_type=MESH)

    def part_copy(step):
        return pltpu.make_async_remote_copy(
            src_ref=acc.at[step], dst_ref=parts.at[step], send_sem=part_send.at[step], recv_sem=part_recv.at[step],
            device_id=(blk, lax.rem(col + nc - step, nc)), device_id_type=MESH)

    def run(action):
        def body(step, carry):
            action(step)
            return carry
        return body

    lax.fori_loop(1, nc, run(lambda step: row_copy(step).start()), 0)
    lax.fori_loop(1, nb, run(lambda step: col_copy(step).start()), 0)

    def put_row(step, points):
        rows[:DEPTH, pl.ds(pl.multiple_of(step * WIDTH, WIDTH), WIDTH)] = row_side(points).astype(BF16)

    def put_col(step, block):
        at = pl.ds(pl.multiple_of(step * WIDTH, WIDTH), WIDTH)
        tall = jnp.concatenate([col_side(block[:FEAT]), jnp.zeros((WIDTH - DEPTH, WIDTH), F32)], axis=0)
        cols_t[at, :] = tall.T.astype(BF16)
        high = block[FEAT:].astype(BF16)
        vecs[:PROBES, at] = high
        vecs[PROBES:, at] = (block[FEAT:] - high.astype(F32)).astype(BF16)

    rows[DEPTH:, :] = jnp.zeros((WIDTH - DEPTH, nc * WIDTH), BF16)
    put_row(0, mine[:FEAT])
    put_col(0, mine[...])

    def arrived_row(step, carry):
        row_copy(step).wait_recv()
        put_row(step, rowbuf[step])
        return carry

    lax.fori_loop(1, nc, arrived_row, 0)

    def arrived_col(step):
        col_copy(step).wait_recv()
        put_col(step, colbuf[step])

    def sums(first_col, col_count, first_row, row_count):
        at = pl.ds(pl.multiple_of(first_col * WIDTH, WIDTH), col_count * WIDTH)
        rows_at = pl.ds(pl.multiple_of(first_row * WIDTH, WIDTH), row_count * WIDTH)
        return tile_sums(cols_t[at, :], vecs[:, at], rows[:, rows_at])

    half = nb // 2

    def strip(pair, carry):
        @pl.when(pair > 0)
        def _():
            arrived_col(2 * pair)
        arrived_col(2 * pair + 1)
        total = sums(2 * pair, 2, 0, nc)
        for k in range(nc):
            acc[k] += total[:, k * WIDTH:(k + 1) * WIDTH]
        return carry

    lax.fori_loop(0, half // 2, strip, 0)
    lax.fori_loop(half, nb, run(arrived_col), 0)

    def chunk(turn, carry):
        first = nc - 2 - 2 * turn
        total = sums(half, nb - half, first, 2)
        for k in range(2):
            acc[first + k] += total[:, k * WIDTH:(k + 1) * WIDTH]
        part_copy(first + 1).start()

        @pl.when(first > 0)
        def _():
            part_copy(first).start()
        return carry

    lax.fori_loop(0, nc // 2, chunk, 0)
    lax.fori_loop(1, nc, run(lambda step: row_copy(step).wait_send()), 0)
    lax.fori_loop(1, nb, run(lambda step: col_copy(step).wait_send()), 0)
    lax.fori_loop(1, nc, run(lambda step: part_copy(step).wait_send()), 0)

    def add_part(step, total):
        part_copy(step).wait_recv()
        return total + parts[step]

    out_ref[...] = lax.fori_loop(1, nc, add_part, acc[0])


def on_device(nb, nc, features, vectors, lengthscales, noise_var, signal):
    sums = pl.pallas_call(
        functools.partial(kernel, nb, nc),
        out_shape=jax.ShapeDtypeStruct((PROBES, WIDTH), F32),
        in_specs=[
            pl.BlockSpec(memory_space=pltpu.SMEM),
            pl.BlockSpec(memory_space=pltpu.VMEM),
            pl.BlockSpec(memory_space=pltpu.VMEM),
        ],
        out_specs=pl.BlockSpec(memory_space=pltpu.VMEM),
        scratch_shapes=[
            pltpu.VMEM((FEAT + PROBES, WIDTH), F32),
            pltpu.VMEM((nb, FEAT + PROBES, WIDTH), F32),
            pltpu.VMEM((nc, FEAT, WIDTH), F32),
            pltpu.VMEM((WIDTH, nc * WIDTH), BF16),
            pltpu.VMEM((nb * WIDTH, WIDTH), BF16),
            pltpu.VMEM((2 * PROBES, nb * WIDTH), BF16),
            pltpu.VMEM((nc, PROBES, WIDTH), F32),
            pltpu.VMEM((nc, PROBES, WIDTH), F32),
            pltpu.SemaphoreType.DMA((nc,)),
            pltpu.SemaphoreType.DMA((nc,)),
            pltpu.SemaphoreType.DMA((nb,)),
            pltpu.SemaphoreType.DMA((nb,)),
            pltpu.SemaphoreType.DMA((nc,)),
            pltpu.SemaphoreType.DMA((nc,)),
        ],
        compiler_params=pltpu.CompilerParams(
            collective_id=0, has_side_effects=True, vmem_limit_bytes=48 * 1024 * 1024
        ),
        name="matern_sums",
    )(lengthscales, features, vectors)
    return signal[0] * sums + noise_var[None, :] * vectors


def solution(mesh):
    nb, nc = mesh.shape["blk"], mesh.shape["col"]
    placed = (P(None, ("blk", "col")), P(None, ("blk", "col")), P(), P(("blk", "col")), P())
    return jax.shard_map(
        functools.partial(on_device, nb, nc),
        mesh=mesh,
        in_specs=placed,
        out_specs=P(None, ("blk", "col")),
        check_vma=False,
    )
```

time: 598 us -> 52.4 us (0.09); the launches traced: 586 us -> 52.2 us
  matrix products: 181 us -> 0 us
  waiting for transfers between devices: 174 us -> 0 us
  starting transfers between devices: 141 us -> 0 us
  blocking collectives: 52.7 us -> 0 us
  Pallas kernels: 0 us -> 48.9 us
  between operations: 14.1 us -> 0.68 us
  local copies, waits for them, and re-layouts: 13.5 us -> 2.03 us
  loops' own time: 6.67 us -> 0 us
    dot_general x784 -> x0, matrix products: 181 us -> none  [the longest x272 91.2 us: matern_tile(): lax.dot_general(rows_x, cols_x, (((0,), (0,)), ((), ())), precision=lax.P...]
    ppermute x48 -> x0, starting transfers between devices: 141 us -> none  [shifted(): return lax.ppermute(value, axis, pairs)]
    psum x1 -> x0, waiting for transfers between devices: 121 us -> none  [on_device(): whole_rows = lax.psum(row_sums, 'col')]
    all_gather x2 -> x0, blocking collectives: 52.7 us -> none  [the longest x1 29.8 us: on_device(): lax.all_gather(vectors, 'col', axis=1, tiled=True)]
    ppermute x48 -> x0, waiting for transfers between devices: 52.5 us -> none  [shifted(): return lax.ppermute(value, axis, pairs)]
    pallas_call x0 -> x1, Pallas kernels: none -> 48.9 us  [on_device(): pl.pallas_call(functools.partial(kernel, nb, nc), out_shape=jax.ShapeDtyp...]
    add x272 -> x0, local copies, waits for them, and re-layouts: 12.6 us -> none  [matern_tile(): rows_sq[:, None] + cols_sq[None, :] - 2.0 * cross]
    another operation x18 -> x0, loops' own time: 6.67 us -> none  [the longest x17 5.05 us: tile_sums(): lax.scan(one_group, start, (group_x, group_sq, group_v))]
  transfers between devices with their start and end apart: 49 -> 0, of which waited for: 23 -> 0; matrix products, arithmetic and copies ran while one was open for 30% -> 0% of each run, Pallas kernels for 0% -> 0%
where the time goes in v1:
time: 52.4 us; the launch traced here: 52.2 us
  Pallas kernels  48.9 us (93%)
  local copies, waits for them, and re-layouts  2.03 us (4%)
  between operations  0.68 us (1%)
  other arithmetic  0.6 us (1%)
    pallas_call x1, Pallas kernels, on_device(): pl.pallas_call(functools.partial(kernel, nb, nc), out_shape=jax.ShapeDtyp...  48.9 us
    unnamed x8, local copies, waits for them, and re-layouts  2.03 us

profile of v1, /device:TPU:1, one launch (start us, length us, event | category | flops | bytes accessed | tf_op | source)
XLA Modules:
  0.0 52.2 jit_solution(10711233148169260203)
XLA Ops:
  0.7 0.0 copy-start.2
  0.7 0.6 %copy-done.2 = f32[8]{0:T(128)S(1)} copy-done((f32[8]{0:T(128)S(1)}, f32[8]{0:T(128)}, u32[]{:S(2)}) %copy-start.2) | copy-done | bytes 56
  1.3 0.0 copy-start
  1.3 0.7 %copy-done = f32[16,128]{1,0:T(8,128)S(1)} copy-done((f32[16,128]{1,0:T(8,128)S(1)}, f32[16,128]{1,0:T(8,128)}, u32[]{:S(2)}) %copy-start) | copy-done | bytes 8216
  2.0 0.0 copy-start.1
  2.0 0.7 %copy-done.1 = f32[8,128]{1,0:T(8,128)S(1)} copy-done((f32[8,128]{1,0:T(8,128)S(1)}, f32[8,128]{1,0:T(8,128)}, u32[]{:S(2)}) %copy-start.1) | copy-done | bytes 4120
  2.7 0.0 copy-start.3
  2.7 48.9 %matern_sums.1 = f32[16,128]{1,0:T(8,128)S(1)} custom-call(f32[8]{0:T(128)S(1)} %copy-done.2, f32[8,128]{1,0:T(8,128)S(1)} %copy-done.1, f32[16,128]{1,0:T(8,128)S(1)} %copy-done), custom_call_target="tpu_custom_call" | custom-call | tf_op jit(solution)/shard_map/matern_sums/pallas_call | solution.py:194
  51.6 0.0 copy-done.3
  51.6 0.6 %multiply_add_fusion = f32[16,128]{1,0:T(8,128)} fusion(f32[16,128]{1,0:T(8,128)S(1)} %copy-done, f32[16,128]{1,0:T(8,128)S(1)} %matern_sums.1, f32[128]{0:T(128)S(1)} %copy-done.3, f32[]{:T(128)} %bitcast.1), kind=kLoop, calls=%fused_computation | loop fusion | flops 6144 | bytes 25092 | tf_op jit(solution)/shard_map/add | solution.py:224
Async XLA Ops:
  0.7 0.7 %copy-start.2 = (f32[8]{0:T(128)S(1)}, f32[8]{0:T(128)}, u32[]{:S(2)}) copy-start(f32[8]{0:T(128)} %ls_ref.1) | copy-start | bytes 100
  1.3 0.7 %copy-start = (f32[16,128]{1,0:T(8,128)S(1)}, f32[16,128]{1,0:T(8,128)}, u32[]{:S(2)}) copy-start(f32[16,128]{1,0:T(8,128)} %vec_ref.1) | copy-start | bytes 24580
  2.0 0.7 %copy-start.1 = (f32[8,128]{1,0:T(8,128)S(1)}, f32[8,128]{1,0:T(8,128)}, u32[]{:S(2)}) copy-start(f32[8,128]{1,0:T(8,128)} %feat_ref.1) | copy-start | bytes 12292
  2.7 48.9 %copy-start.3 = (f32[128]{0:T(128)S(1)}, f32[128]{0:T(128)}, u32[]{:S(2)}) copy-start(f32[128]{0:T(128)} %param.8) | copy-start | bytes 1540

commit v2 on v1

v2 whole, which is shorter than its diff:
```python
import functools
import math

import jax
import jax.numpy as jnp
from jax import lax
from jax.experimental import pallas as pl
from jax.experimental.pallas import tpu as pltpu
from jax.sharding import PartitionSpec as P

MESH = pl.DeviceIdType.MESH
F32 = jnp.float32
BF16 = jnp.bfloat16
SCALE = math.sqrt(5.0 / 3.0)
HALF3 = math.sqrt(3.0) / 2.0
RATE = -math.sqrt(3.0) * math.log2(math.e)
TINY = 1e-30
WIDTH = 128
FEAT = 8
PROBES = 16
DEPTH = 64


def split3(value):
    high = value.astype(BF16).astype(F32)
    rest = value - high
    mid = rest.astype(BF16).astype(F32)
    return high, mid, rest - mid


def norms3(points):
    return split3(jnp.sum(points * points, axis=0, keepdims=True))


def row_side(points):
    high, mid, low = split3(points)
    nh, nm, nl = norms3(points)
    one, zero = jnp.ones_like(nh), jnp.zeros_like(nh)
    extra = jnp.concatenate([nh, nm, nl, one, one, one, zero, zero], axis=0)
    pad = jnp.zeros_like(points)
    return jnp.concatenate([high, high, mid, mid, high, low, extra, pad], axis=0)


def col_side(points):
    high, mid, low = (-2.0 * part for part in split3(points))
    nh, nm, nl = norms3(points)
    one, zero = jnp.ones_like(nh), jnp.zeros_like(nh)
    extra = jnp.concatenate([one, one, one, nh, nm, nl, zero, zero], axis=0)
    pad = jnp.zeros_like(points)
    return jnp.concatenate([high, mid, high, mid, low, high, extra, pad], axis=0)


def matern(dist_sq):
    floor = jnp.maximum(dist_sq, TINY)
    dist = floor * lax.rsqrt(floor)
    decay = jnp.exp2(dist * RATE)
    shifted = dist + HALF3
    return (shifted * shifted + 0.25) * decay


def halves(value):
    high = value.astype(BF16)
    return high, (value - high.astype(F32)).astype(BF16)


def fold(both):
    return both[:PROBES] + both[PROBES:]


def times(vecs, high, low, dims):
    first = lax.dot_general(vecs, high, dims, preferred_element_type=F32)
    return fold(first) + lax.dot_general(vecs[:PROBES], low, dims, preferred_element_type=F32)


OVER_ROWS = (((1,), (0,)), ((), ()))
OVER_COLS = (((1,), (1,)), ((), ()))


def kernel(nb, nc, ls_ref, feat_ref, vec_ref, out_ref, rowbuf, colbuf, rows_t, row_vecs, cols, col_vecs,
           row_acc, col_acc, row_parts, col_parts, dist0, dist1, high0, high1, low0, low1,
           row_send, row_recv, col_send, col_recv, rp_send, rp_recv, cp_send, cp_recv):
    blk, col = lax.axis_index("blk"), lax.axis_index("col")
    half = nb // 2
    pairs, chunks = half // 2, nc // 2
    dist, highs, lows = (dist0, dist1), (high0, high1), (low0, low1)
    mine = rowbuf.at[0]

    def loop(first, last, action):
        def body(step, carry):
            action(step)
            return carry
        lax.fori_loop(first, last, body, 0)

    def row_peer(step):
        return (blk, lax.rem(col + step, nc))

    def row_owner(step):
        return (blk, lax.rem(col + nc - step, nc))

    def col_peer(step):
        return (lax.rem(blk + step, nb), col)

    def col_owner(step):
        return (lax.rem(blk + nb - step, nb), col)

    barrier = pltpu.get_barrier_semaphore()

    def greet(peer):
        return lambda step: pl.semaphore_signal(barrier, inc=1, device_id=peer(step), device_id_type=MESH)

    loop(1, nc, greet(row_owner))
    loop(1, half + 1, greet(col_owner))

    feature = lax.broadcasted_iota(jnp.int32, (FEAT, WIDTH), 0)
    lengths = jnp.full((FEAT, WIDTH), ls_ref[0], F32)
    for k in range(1, FEAT):
        lengths = jnp.where(feature == k, ls_ref[k], lengths)
    scaled = feat_ref[...] / lengths * SCALE
    rowbuf[0, :FEAT] = scaled
    rowbuf[0, FEAT:] = vec_ref[...]
    colbuf[half - 1, :FEAT] = scaled
    colbuf[half - 1, FEAT:] = vec_ref[...]
    colbuf[half + 1] = jnp.zeros((FEAT + PROBES, WIDTH), F32)
    row_acc[...] = jnp.zeros_like(row_acc)
    col_acc[...] = jnp.zeros_like(col_acc)
    high1[...] = jnp.zeros_like(high1)
    low1[...] = jnp.zeros_like(low1)
    cols[DEPTH:, :] = jnp.zeros((WIDTH - DEPTH, cols.shape[1]), BF16)
    pl.semaphore_wait(barrier, nc - 1 + half)

    def row_copy(step):
        return pltpu.make_async_remote_copy(
            src_ref=mine, dst_ref=rowbuf.at[step], send_sem=row_send.at[step], recv_sem=row_recv.at[step],
            device_id=row_peer(step), device_id_type=MESH)

    def col_copy(place):
        return pltpu.make_async_remote_copy(
            src_ref=mine, dst_ref=colbuf.at[place], send_sem=col_send.at[place], recv_sem=col_recv.at[place],
            device_id=col_peer(jnp.where(place == half, half, place + 1)), device_id_type=MESH)

    def row_part(step):
        return pltpu.make_async_remote_copy(
            src_ref=row_acc.at[step], dst_ref=row_parts.at[step], send_sem=rp_send.at[step], recv_sem=rp_recv.at[step],
            device_id=row_owner(step), device_id_type=MESH)

    def col_part(place):
        return pltpu.make_async_remote_copy(
            src_ref=col_acc.at[place], dst_ref=col_parts.at[place], send_sem=cp_send.at[place],
            recv_sem=cp_recv.at[place], device_id=col_owner(place + 1), device_id_type=MESH)

    loop(1, nc, lambda step: row_copy(step).start())
    loop(0, half - 1, lambda place: col_copy(place).start())
    col_copy(half).start()

    def span(place, count):
        return pl.ds(pl.multiple_of(place * WIDTH, WIDTH), count * WIDTH)

    def put_cols(pair):
        for k in range(2):
            block = colbuf[2 * pair + k]
            at = span(2 * pair + k, 1)
            cols[:DEPTH, at] = col_side(block[:FEAT]).astype(BF16)
            share = jnp.where(2 * pair + k == half - 1, 0.5, 1.0)
            high, low = halves(block[FEAT:] * share)
            col_vecs[:PROBES, at] = high
            col_vecs[PROBES:, at] = low

    def inner(place, count, chunk, into):
        at = pl.ds(chunk * 2 * WIDTH, 2 * WIDTH)
        into[:, :count * WIDTH] = jnp.dot(rows_t[at, :], cols[:, span(place, count)], preferred_element_type=F32)

    def elementwise(which, count):
        at = slice(0, count * WIDTH)
        high, low = halves(matern(dist[which][:, at]))
        highs[which][:, at] = high
        lows[which][:, at] = low

    def add_rows(place, count, chunk, which):
        at = slice(0, count * WIDTH)
        total = times(col_vecs[:, span(place, count)], highs[which][:, at], lows[which][:, at], OVER_COLS)
        for k in range(2):
            row_acc[2 * chunk + k] += total[:, k * WIDTH:(k + 1) * WIDTH]

    def add_cols(place, chunk, which):
        total = times(row_vecs[:, chunk * 2 * WIDTH:(chunk + 1) * 2 * WIDTH], highs[which][...], lows[which][...], OVER_ROWS)
        for k in range(2):
            col_acc[place + k] += total[:, k * WIDTH:(k + 1) * WIDTH]

    loop(1, nc, lambda step: row_copy(step).wait_recv())
    for step in range(nc):
        at = slice(step * WIDTH, (step + 1) * WIDTH)
        tall = jnp.concatenate([row_side(rowbuf[step, :FEAT]), jnp.zeros((WIDTH - DEPTH, WIDTH), F32)], axis=0)
        rows_t[at, :] = tall.T.astype(BF16)
        high, low = halves(rowbuf[step, FEAT:])
        row_vecs[:PROBES, at] = high
        row_vecs[PROBES:, at] = low
    col_copy(0).wait_recv()
    col_copy(1).wait_recv()
    put_cols(0)
    inner(0, 2, 0, dist[0])

    def one_pair(pair):
        col_copy(2 * pair + 2).wait_recv()

        @pl.when(pair < pairs - 2)
        def _():
            col_copy(2 * pair + 3).wait_recv()
        put_cols(pair + 1)
        for chunk in range(chunks):
            now, other = chunk % 2, (chunk + 1) % 2
            if chunk + 1 < chunks:
                inner(2 * pair, 2, chunk + 1, dist[other])
            else:
                inner(2 * pair + 2, 2, 0, dist[other])
            elementwise(now, 2)
            before = 2 * pair if chunk > 0 else 2 * jnp.maximum(pair - 1, 0)
            add_cols(before, (chunk - 1) % chunks, other)
            add_rows(before, 2, (chunk - 1) % chunks, other)

        @pl.when(pair > 0)
        def _():
            col_part(2 * pair - 2).start()
            col_part(2 * pair - 1).start()

    loop(0, pairs, one_pair)
    for chunk in range(chunks + 1):
        now, other = chunk % 2, (chunk + 1) % 2
        if chunk + 1 < chunks:
            inner(half, 1, chunk + 1, dist[other])
        if chunk < chunks:
            elementwise(now, 1)
        if chunk == 0:
            add_cols(half - 2, chunks - 1, other)
            add_rows(half - 2, 2, chunks - 1, other)
            col_part(half - 2).start()
        else:
            add_rows(half, 1, chunk - 1, other)
            if chunk > 1:
                row_part(2 * chunk - 2).start()
            row_part(2 * chunk - 1).start()

    loop(1, nc, lambda step: row_copy(step).wait_send())
    loop(0, half - 1, lambda place: col_copy(place).wait_send())
    col_copy(half).wait_send()
    loop(0, half - 1, lambda place: col_part(place).wait_send())
    loop(1, nc, lambda step: row_part(step).wait_send())

    def add_col_part(place, total):
        col_part(place).wait_recv()
        return total + col_parts[place]

    def add_row_part(step, total):
        row_part(step).wait_recv()
        return total + row_parts[step]

    total = row_acc[0] + 0.5 * col_acc[half - 1]
    total = lax.fori_loop(0, half - 1, add_col_part, total)
    out_ref[...] = lax.fori_loop(1, nc, add_row_part, total)


def on_device(nb, nc, features, vectors, lengthscales, noise_var, signal):
    half = nb // 2
    sums = pl.pallas_call(
        functools.partial(kernel, nb, nc),
        out_shape=jax.ShapeDtypeStruct((PROBES, WIDTH), F32),
        in_specs=[
            pl.BlockSpec(memory_space=pltpu.SMEM),
            pl.BlockSpec(memory_space=pltpu.VMEM),
            pl.BlockSpec(memory_space=pltpu.VMEM),
        ],
        out_specs=pl.BlockSpec(memory_space=pltpu.VMEM),
        scratch_shapes=[
            pltpu.VMEM((nc, FEAT + PROBES, WIDTH), F32),
            pltpu.VMEM((half + 2, FEAT + PROBES, WIDTH), F32),
            pltpu.VMEM((nc * WIDTH, WIDTH), BF16),
            pltpu.VMEM((2 * PROBES, nc * WIDTH), BF16),
            pltpu.VMEM((WIDTH, (half + 2) * WIDTH), BF16),
            pltpu.VMEM((2 * PROBES, (half + 2) * WIDTH), BF16),
            pltpu.VMEM((nc, PROBES, WIDTH), F32),
            pltpu.VMEM((half, PROBES, WIDTH), F32),
            pltpu.VMEM((nc, PROBES, WIDTH), F32),
            pltpu.VMEM((half, PROBES, WIDTH), F32),
        ]
        + [pltpu.VMEM((2 * WIDTH, 2 * WIDTH), F32)] * 2
        + [pltpu.VMEM((2 * WIDTH, 2 * WIDTH), BF16)] * 4
        + [pltpu.SemaphoreType.DMA((count,)) for count in (nc, nc, half + 1, half + 1, nc, nc, half, half)],
        compiler_params=pltpu.CompilerParams(
            collective_id=0, has_side_effects=True, vmem_limit_bytes=48 * 1024 * 1024
        ),
        name="matern_sums",
    )(lengthscales, features, vectors)
    return signal[0] * sums + noise_var[None, :] * vectors


def solution(mesh):
    nb, nc = mesh.shape["blk"], mesh.shape["col"]
    placed = (P(None, ("blk", "col")), P(None, ("blk", "col")), P(), P(("blk", "col")), P())
    return jax.shard_map(
        functools.partial(on_device, nb, nc),
        mesh=mesh,
        in_specs=placed,
        out_specs=P(None, ("blk", "col")),
        check_vma=False,
    )
```

time: 52.4 us -> 44.9 us (0.86)
  Pallas kernels: 48.9 us -> 41.1 us
    pallas_call x1, Pallas kernels: 48.9 us -> 41.1 us  [on_device(): pl.pallas_call(functools.partial(kernel, nb, nc), out_shape=jax.ShapeDtyp...]
where the time goes in v2:
time: 44.9 us; the launch traced here: 44.4 us
  Pallas kernels  41.1 us (92%)
  local copies, waits for them, and re-layouts  2.03 us (5%)
  between operations  0.68 us (2%)
  other arithmetic  0.6 us (1%)
    pallas_call x1, Pallas kernels, on_device(): pl.pallas_call(functools.partial(kernel, nb, nc), out_shape=jax.ShapeDtyp...  41.1 us
    unnamed x8, local copies, waits for them, and re-layouts  2.03 us

profile of v2, /device:TPU:1, one launch (start us, length us, event | category | flops | bytes accessed | tf_op | source)
XLA Modules:
  0.0 44.4 jit_solution(14678059303780878894)
XLA Ops:
  0.7 0.0 copy-start.2
  0.7 0.6 %copy-done.2 = f32[8]{0:T(128)S(1)} copy-done((f32[8]{0:T(128)S(1)}, f32[8]{0:T(128)}, u32[]{:S(2)}) %copy-start.2) | copy-done | bytes 56
  1.3 0.0 copy-start
  1.3 0.7 %copy-done = f32[16,128]{1,0:T(8,128)S(1)} copy-done((f32[16,128]{1,0:T(8,128)S(1)}, f32[16,128]{1,0:T(8,128)}, u32[]{:S(2)}) %copy-start) | copy-done | bytes 8216
  2.0 0.0 copy-start.1
  2.0 0.7 %copy-done.1 = f32[8,128]{1,0:T(8,128)S(1)} copy-done((f32[8,128]{1,0:T(8,128)S(1)}, f32[8,128]{1,0:T(8,128)}, u32[]{:S(2)}) %copy-start.1) | copy-done | bytes 4120
  2.7 0.0 copy-start.3
  2.7 41.1 %matern_sums.1 = f32[16,128]{1,0:T(8,128)S(1)} custom-call(f32[8]{0:T(128)S(1)} %copy-done.2, f32[8,128]{1,0:T(8,128)S(1)} %copy-done.1, f32[16,128]{1,0:T(8,128)S(1)} %copy-done), custom_call_target="tpu_custom_call" | custom-call | tf_op jit(solution)/shard_map/matern_sums/pallas_call | solution.py:263
  43.8 0.0 copy-done.3
  43.8 0.6 %multiply_add_fusion = f32[16,128]{1,0:T(8,128)} fusion(f32[16,128]{1,0:T(8,128)S(1)} %copy-done, f32[16,128]{1,0:T(8,128)S(1)} %matern_sums.1, f32[128]{0:T(128)S(1)} %copy-done.3, f32[]{:T(128)} %bitcast.1), kind=kLoop, calls=%fused_computation | loop fusion | flops 6144 | bytes 25092 | tf_op jit(solution)/shard_map/add | solution.py:292
Async XLA Ops:
  0.7 0.7 %copy-start.2 = (f32[8]{0:T(128)S(1)}, f32[8]{0:T(128)}, u32[]{:S(2)}) copy-start(f32[8]{0:T(128)} %ls_ref.1) | copy-start | bytes 100
  1.3 0.7 %copy-start = (f32[16,128]{1,0:T(8,128)S(1)}, f32[16,128]{1,0:T(8,128)}, u32[]{:S(2)}) copy-start(f32[16,128]{1,0:T(8,128)} %vec_ref.1) | copy-start | bytes 24580
  2.0 0.7 %copy-start.1 = (f32[8,128]{1,0:T(8,128)S(1)}, f32[8,128]{1,0:T(8,128)}, u32[]{:S(2)}) copy-start(f32[8,128]{1,0:T(8,128)} %feat_ref.1) | copy-start | bytes 12292
  2.7 41.1 %copy-start.3 = (f32[128]{0:T(128)S(1)}, f32[128]{0:T(128)}, u32[]{:S(2)}) copy-start(f32[128]{0:T(128)} %param.8) | copy-start | bytes 1540

commit v3 on v2

v3 whole, which is shorter than its diff:
```python
import functools
import math

import jax
import jax.numpy as jnp
from jax import lax
from jax.experimental import pallas as pl
from jax.experimental.pallas import tpu as pltpu
from jax.sharding import PartitionSpec as P

MESH = pl.DeviceIdType.MESH
F32 = jnp.float32
BF16 = jnp.bfloat16
SCALE = math.sqrt(5.0 / 3.0)
HALF3 = math.sqrt(3.0) / 2.0
RATE = -math.sqrt(3.0) * math.log2(math.e)
TINY = 1e-30
WIDTH = 128
FEAT = 8
PROBES = 16
DEPTH = 64


def split3(value):
    high = value.astype(BF16).astype(F32)
    rest = value - high
    mid = rest.astype(BF16).astype(F32)
    return high, mid, rest - mid


def norms3(points):
    return split3(jnp.sum(points * points, axis=0, keepdims=True))


def row_side(points):
    high, mid, low = split3(points)
    nh, nm, nl = norms3(points)
    one, zero = jnp.ones_like(nh), jnp.zeros_like(nh)
    extra = jnp.concatenate([nh, nm, nl, one, one, one, zero, zero], axis=0)
    pad = jnp.zeros_like(points)
    return jnp.concatenate([high, high, mid, mid, high, low, extra, pad], axis=0)


def col_side(points):
    high, mid, low = (-2.0 * part for part in split3(points))
    nh, nm, nl = norms3(points)
    one, zero = jnp.ones_like(nh), jnp.zeros_like(nh)
    extra = jnp.concatenate([one, one, one, nh, nm, nl, zero, zero], axis=0)
    pad = jnp.zeros_like(points)
    return jnp.concatenate([high, mid, high, mid, low, high, extra, pad], axis=0)


def matern(dist_sq):
    floor = jnp.maximum(dist_sq, TINY)
    dist = floor * lax.rsqrt(floor)
    decay = jnp.exp2(dist * RATE)
    shifted = dist + HALF3
    return (shifted * shifted + 0.25) * decay


def halves(value):
    high = value.astype(BF16)
    return high, (value - high.astype(F32)).astype(BF16)


def fold(both):
    return both[:PROBES] + both[PROBES:]


def times(vecs, high, low, dims):
    first = lax.dot_general(vecs, high, dims, preferred_element_type=F32)
    return fold(first) + lax.dot_general(vecs[:PROBES], low, dims, preferred_element_type=F32)


OVER_ROWS = (((1,), (0,)), ((), ()))
OVER_COLS = (((1,), (1,)), ((), ()))


def kernel(nb, nc, ls_hbm, feat_hbm, vec_hbm, out_ref, lengthscales, rowbuf, colbuf, rows_t, row_vecs, cols,
           col_vecs, row_acc, col_acc, row_parts, col_parts, dist0, dist1, high0, high1, low0, low1,
           in_sem, row_send, row_recv, relay_send, relay_recv, col_send, col_recv, rp_send, rp_recv, cp_send, cp_recv):
    half = nb // 2
    pairs, chunks, ring = half // 2, nc // 2, nc // 2
    dist, highs, lows = (dist0, dist1), (high0, high1), (low0, low1)
    blk, col = lax.axis_index("blk"), lax.axis_index("col")
    core = blk % 2
    group, chip = blk - core + col % 2, col // 2

    def device(group, chip, core):
        return (group - group % 2 + core, 2 * chip + group % 2)

    own = colbuf.at[half]
    loads = [
        pltpu.make_async_copy(ls_hbm, lengthscales, in_sem.at[0]),
        pltpu.make_async_copy(feat_hbm, own.at[:FEAT], in_sem.at[1]),
        pltpu.make_async_copy(vec_hbm, own.at[FEAT:], in_sem.at[2]),
    ]
    for load in loads:
        load.start()

    def loop(first, last, action):
        def body(step, carry):
            action(step)
            return carry
        lax.fori_loop(first, last, body, 0)

    def row_offset(step):
        return (step + 1) // 2 if step % 2 else ring - step // 2

    def row_peer(step):
        return device(group, (chip + row_offset(step)) % ring, core)

    def row_owner(step, other):
        return device(group, (chip + ring - row_offset(step)) % ring, 1 - core if other else core)

    def col_offset(place):
        return jnp.where(place % 2 == 0, place + 1, nb - 1 - place)

    def col_peer(place):
        return device((group + col_offset(place)) % nb, chip, core)

    def col_owner(place):
        return device((group + nb - col_offset(place)) % nb, chip, core)

    sibling = device(group, chip, 1 - core)
    barrier = pltpu.get_barrier_semaphore()

    def greet(peer):
        pl.semaphore_signal(barrier, inc=1, device_id=peer, device_id_type=MESH)

    greet(sibling)
    for step in range(1, ring):
        greet(row_owner(step, False))
    loop(0, half, lambda place: greet(col_owner(place)))

    row_acc[...] = jnp.zeros_like(row_acc)
    col_acc[...] = jnp.zeros_like(col_acc)
    cols[DEPTH:, :] = jnp.zeros((WIDTH - DEPTH, cols.shape[1]), BF16)
    for load in loads:
        load.wait()
    feature = lax.broadcasted_iota(jnp.int32, (FEAT, WIDTH), 0)
    lengths = jnp.full((FEAT, WIDTH), lengthscales[0], F32)
    for k in range(1, FEAT):
        lengths = jnp.where(feature == k, lengthscales[k], lengths)
    own[:FEAT] = own[:FEAT] / lengths * SCALE
    rowbuf[0, 0] = own[...]
    high1[...] = jnp.zeros_like(high1)
    low1[...] = jnp.zeros_like(low1)
    pl.semaphore_wait(barrier, ring + half)

    def push(source, target, send, recv, device):
        return pltpu.make_async_remote_copy(
            src_ref=source, dst_ref=target, send_sem=send, recv_sem=recv, device_id=device, device_id_type=MESH)

    def row_copy(step):
        return push(own, rowbuf.at[0, step], row_send, row_recv.at[step], row_peer(step))

    def row_relay(step):
        source = rowbuf.at[0, step] if step else own
        return push(source, rowbuf.at[1, step], relay_send, relay_recv.at[step // (ring // 2)], sibling)

    def col_copy(place):
        return push(own, colbuf.at[place], col_send, col_recv.at[place // 2], col_peer(place))

    def row_part(slot):
        return push(row_acc.at[slot], row_parts.at[slot - 1], rp_send, rp_recv, row_owner(slot // 2, slot % 2))

    def col_part(place):
        return push(col_acc.at[place], col_parts.at[place], cp_send, cp_recv, col_owner(place))

    def await_all(region, sem):
        pltpu.make_async_copy(region, region, sem).wait()

    row_relay(0).start()
    for step in range(1, ring // 2):
        row_copy(step).start()
    loop(0, half // 2, lambda place: col_copy(place).start())
    for step in range(ring // 2, ring):
        row_copy(step).start()
    loop(half // 2, half, lambda place: col_copy(place).start())

    def span(place, count):
        return pl.ds(pl.multiple_of(place * WIDTH, WIDTH), count * WIDTH)

    def put_col(place):
        block = colbuf[place]
        at = span(place, 1)
        cols[:DEPTH, at] = col_side(block[:FEAT]).astype(BF16)
        high, low = halves(block[FEAT:])
        col_vecs[:PROBES, at] = high
        col_vecs[PROBES:, at] = low

    def get_pair(pair):
        await_all(colbuf.at[pl.ds(2 * pair, 2)], col_recv.at[pair])
        put_col(2 * pair)
        put_col(2 * pair + 1)

    def pass_rows(side):
        for step in range(side * ring // 2, (side + 1) * ring // 2):
            if step:
                await_all(rowbuf.at[0, step], row_recv.at[step])
                row_relay(step).start()

    def get_rows(side):
        first = side * ring // 2
        await_all(rowbuf.at[1, first:first + ring // 2], relay_recv.at[side])
        for slot in range(2 * first, 2 * first + ring):
            at = slice(slot * WIDTH, (slot + 1) * WIDTH)
            block = rowbuf.at[slot % 2, slot // 2]
            tall = jnp.concatenate([row_side(block[:FEAT]), jnp.zeros((WIDTH - DEPTH, WIDTH), F32)], axis=0)
            rows_t[at, :] = tall.T.astype(BF16)
            high, low = halves(block[FEAT:])
            row_vecs[:PROBES, at] = high
            row_vecs[PROBES:, at] = low

    def inner(slot, place, count, even):
        dist[even][:, :count * WIDTH] = jnp.dot(
            rows_t[span(slot, 2), :], cols[:, span(place, count)], preferred_element_type=F32)

    def elementwise(count, even):
        at = slice(0, count * WIDTH)
        high, low = halves(matern(dist[even][:, at]))
        highs[even][:, at] = high
        lows[even][:, at] = low

    def add_rows(slot, place, even):
        total = times(col_vecs[:, span(place, 2)], highs[even][...], lows[even][...], OVER_COLS)
        for k in range(2):
            row_acc[slot + k] += total[:, k * WIDTH:(k + 1) * WIDTH]

    def add_cols(slot, place, count, even):
        at = slice(0, count * WIDTH)
        total = times(row_vecs[:, span(slot, 2)], highs[even][:, at], lows[even][:, at], OVER_ROWS)
        for k in range(count):
            col_acc[place + k] += total[:, k * WIDTH:(k + 1) * WIDTH]

    quarter, tiles = pairs // 2, nc // 4

    def unit_rows(unit):
        return jnp.where((unit >= quarter) & (unit < 3 * quarter), nc // 2, 0)

    def unit_place(unit):
        return 2 * jnp.where(unit < quarter, unit, jnp.where(unit < 3 * quarter, unit - quarter, unit - 2 * quarter))

    put_col(half)
    pass_rows(0)
    get_rows(0)
    get_pair(0)
    inner(0, 0, 2, 0)

    def one_unit(unit):
        @pl.when((unit < quarter - 1) | ((unit >= 2 * quarter - 1) & (unit < 3 * quarter - 1)))
        def _():
            get_pair(unit_place(unit + 1) // 2)

        @pl.when(unit == quarter // 4)
        def _():
            pass_rows(1)

        @pl.when(unit == quarter - 1)
        def _():
            get_rows(1)

        slots, place = unit_rows(unit), unit_place(unit)
        next_slots = unit_rows(unit + 1)
        next_place = jnp.where(unit == 4 * quarter - 1, half - 2, unit_place(unit + 1))
        old = jnp.maximum(unit - 1, 0)
        old_slots, old_place = unit_rows(old), unit_place(old)
        for tile in range(tiles):
            even, odd = tile % 2, (tile + 1) % 2
            if tile + 1 < tiles:
                inner(slots + 2 * tile + 2, place, 2, odd)
            else:
                inner(next_slots, next_place, 2, odd)
            elementwise(2, even)
            if tile > 0:
                add_cols(slots + 2 * tile - 2, place, 2, odd)
                add_rows(slots + 2 * tile - 2, place, odd)
            else:
                add_cols(old_slots + 2 * tiles - 2, old_place, 2, odd)
                add_rows(old_slots + 2 * tiles - 2, old_place, odd)

        @pl.when(((unit > quarter) & (unit <= 2 * quarter)) | (unit > 3 * quarter))
        def _():
            col_part(old_place).start()
            col_part(old_place + 1).start()

        @pl.when(unit == 3 * quarter)
        def _():
            for slot in range(nc // 2, nc):
                row_part(slot).start()

    loop(0, 4 * quarter, one_unit)
    inner(0, half, 1, 0)
    for chunk in range(chunks + 1):
        even, odd = chunk % 2, (chunk + 1) % 2
        if chunk == 0:
            add_cols(nc // 2 - 2, half - 2, 2, odd)
            add_rows(nc // 2 - 2, half - 2, odd)
            col_part(half - 2).start()
            for slot in range(1, nc // 2):
                row_part(slot).start()
        if chunk + 1 < chunks:
            inner(2 * chunk + 2, half, 1, odd)
        if chunk < chunks:
            elementwise(1, even)
        if chunk > 0:
            add_cols(2 * chunk - 2, half, 1, odd)

    total = row_acc[0] + col_acc[half]
    await_all(col_parts, cp_recv)
    for place in range(half - 1):
        total += col_parts[place]
    await_all(row_parts, rp_recv)
    for slot in range(nc - 1):
        total += row_parts[slot]
    out_ref[...] = total
    await_all(rowbuf.at[0, 1:], row_send)
    await_all(rowbuf.at[1], relay_send)
    await_all(colbuf.at[:half], col_send)
    await_all(row_parts, rp_send)
    await_all(col_parts, cp_send)


def on_device(nb, nc, features, vectors, lengthscales, noise_var, signal):
    half = nb // 2
    sums = pl.pallas_call(
        functools.partial(kernel, nb, nc),
        out_shape=jax.ShapeDtypeStruct((PROBES, WIDTH), F32),
        in_specs=[pl.BlockSpec(memory_space=pltpu.MemorySpace.HBM)] * 3,
        out_specs=pl.BlockSpec(memory_space=pltpu.VMEM),
        scratch_shapes=[
            pltpu.SMEM((FEAT,), F32),
            pltpu.VMEM((2, nc // 2, FEAT + PROBES, WIDTH), F32),
            pltpu.VMEM((half + 1, FEAT + PROBES, WIDTH), F32),
            pltpu.VMEM((nc * WIDTH, WIDTH), BF16),
            pltpu.VMEM((2 * PROBES, nc * WIDTH), BF16),
            pltpu.VMEM((WIDTH, (half + 1) * WIDTH), BF16),
            pltpu.VMEM((2 * PROBES, (half + 1) * WIDTH), BF16),
            pltpu.VMEM((nc, PROBES, WIDTH), F32),
            pltpu.VMEM((half + 1, PROBES, WIDTH), F32),
            pltpu.VMEM((nc - 1, PROBES, WIDTH), F32),
            pltpu.VMEM((half - 1, PROBES, WIDTH), F32),
        ]
        + [pltpu.VMEM((2 * WIDTH, 2 * WIDTH), F32)] * 2
        + [pltpu.VMEM((2 * WIDTH, 2 * WIDTH), BF16)] * 4
        + [
            pltpu.SemaphoreType.DMA((3,)),
            pltpu.SemaphoreType.DMA,
            pltpu.SemaphoreType.DMA((nc // 2,)),
            pltpu.SemaphoreType.DMA,
            pltpu.SemaphoreType.DMA((2,)),
            pltpu.SemaphoreType.DMA,
            pltpu.SemaphoreType.DMA((half // 2,)),
        ]
        + [pltpu.SemaphoreType.DMA] * 4,
        compiler_params=pltpu.CompilerParams(
            collective_id=0, has_side_effects=True, vmem_limit_bytes=60 * 1024 * 1024
        ),
        name="matern_sums",
    )(lengthscales, features, vectors)
    return signal[0] * sums + noise_var[None, :] * vectors


def solution(mesh):
    nb, nc = mesh.shape["blk"], mesh.shape["col"]
    placed = (P(None, ("blk", "col")), P(None, ("blk", "col")), P(), P(("blk", "col")), P())
    return jax.shard_map(
        functools.partial(on_device, nb, nc),
        mesh=mesh,
        in_specs=placed,
        out_specs=P(None, ("blk", "col")),
        check_vma=False,
    )
```

time: 44.9 us -> 41.2 us (0.918)
  Pallas kernels: 41.1 us -> 38.9 us
  local copies, waits for them, and re-layouts: 2.03 us -> 0.01 us
  other arithmetic: 0.6 us -> 1.3 us
    pallas_call x1, Pallas kernels: 41.1 us -> 38.9 us  [on_device(): pl.pallas_call(functools.partial(kernel, nb, nc), out_shape=jax.ShapeDtyp...]
    unnamed x8 -> x4, local copies, waits for them, and re-layouts: 2.03 us -> 0.01 us
    add x1, other arithmetic: 0.6 us -> 1.3 us  [on_device(): return signal[0] * sums + noise_var[None, :] * vectors]
where the time goes in v3:
time: 41.2 us; the launch traced here: 40.9 us
  Pallas kernels  38.9 us (94%)
  other arithmetic  1.3 us (3%)
  between operations  0.69 us (2%)
    pallas_call x1, Pallas kernels, on_device(): pl.pallas_call(functools.partial(kernel, nb, nc), out_shape=jax.ShapeDtyp...  38.9 us
    add x1, other arithmetic, on_device(): return signal[0] * sums + noise_var[None, :] * vectors  1.3 us

profile of v3, /device:TPU:1, one launch (start us, length us, event | category | flops | bytes accessed | tf_op | source)
XLA Modules:
  0.0 40.9 jit_solution(5277694691618380724)
XLA Ops:
  0.7 0.0 copy-start
  0.7 0.0 copy-start.1
  0.7 38.9 %matern_sums.1 = f32[16,128]{1,0:T(8,128)} custom-call(f32[8]{0:T(128)} %ls_hbm.1, f32[8,128]{1,0:T(8,128)} %feat_hbm.1, f32[16,128]{1,0:T(8,128)} %vec_hbm.1), custom_call_target="tpu_custom_call" | custom-call | tf_op jit(solution)/shard_map/matern_sums/pallas_call | solution.py:327
  39.6 0.0 copy-done
  39.6 0.0 copy-done.1
  39.6 1.3 %multiply_add_fusion = f32[16,128]{1,0:T(8,128)} fusion(f32[16,128]{1,0:T(8,128)S(1)} %copy-done, f32[16,128]{1,0:T(8,128)} %matern_sums.1, f32[128]{0:T(128)S(1)} %copy-done.1, f32[]{:T(128)} %bitcast.1), kind=kLoop, calls=%fused_computation | loop fusion | flops 6144 | bytes 25092 | tf_op jit(solution)/shard_map/add | solution.py:362
Async XLA Ops:
  0.7 39.0 %copy-start = (f32[16,128]{1,0:T(8,128)S(1)}, f32[16,128]{1,0:T(8,128)}, u32[]{:S(2)}) copy-start(f32[16,128]{1,0:T(8,128)} %vec_hbm.1) | copy-start | bytes 24580
  0.7 39.0 %copy-start.1 = (f32[128]{0:T(128)S(1)}, f32[128]{0:T(128)}, u32[]{:S(2)}) copy-start(f32[128]{0:T(128)} %param.8) | copy-start | bytes 1540

commit v4 on v3

v4 whole, which is shorter than its diff:
```python
import functools
import math

import jax
import jax.numpy as jnp
from jax import lax
from jax.experimental import pallas as pl
from jax.experimental.pallas import tpu as pltpu
from jax.sharding import PartitionSpec as P

MESH = pl.DeviceIdType.MESH
F32 = jnp.float32
BF16 = jnp.bfloat16
SCALE = math.sqrt(5.0 / 3.0)
HALF3 = math.sqrt(3.0) / 2.0
RATE = -math.sqrt(3.0) * math.log2(math.e)
TINY = 1e-30
WIDTH = 128
FEAT = 8
PROBES = 16
ORDER = (1, 8, 7, 9, 3, 15, 5, 4, 12, 13, 11, 14, 6, 10, 2, 16)
DEPTH = 64


def split3(value):
    high = value.astype(BF16).astype(F32)
    rest = value - high
    mid = rest.astype(BF16).astype(F32)
    return high, mid, rest - mid


def norms3(points):
    return split3(jnp.sum(points * points, axis=0, keepdims=True))


def row_side(points):
    high, mid, low = split3(points)
    nh, nm, nl = norms3(points)
    one, zero = jnp.ones_like(nh), jnp.zeros_like(nh)
    extra = jnp.concatenate([nh, nm, nl, one, one, one, zero, zero], axis=0)
    pad = jnp.zeros_like(points)
    return jnp.concatenate([high, high, mid, mid, high, low, extra, pad], axis=0)


def col_side(points):
    high, mid, low = (-2.0 * part for part in split3(points))
    nh, nm, nl = norms3(points)
    one, zero = jnp.ones_like(nh), jnp.zeros_like(nh)
    extra = jnp.concatenate([one, one, one, nh, nm, nl, zero, zero], axis=0)
    pad = jnp.zeros_like(points)
    return jnp.concatenate([high, mid, high, mid, low, high, extra, pad], axis=0)


def matern(dist_sq):
    floor = jnp.maximum(dist_sq, TINY)
    dist = floor * lax.rsqrt(floor)
    decay = jnp.exp2(dist * RATE)
    shifted = dist + HALF3
    return (shifted * shifted + 0.25) * decay


def halves(value):
    high = value.astype(BF16)
    return high, (value - high.astype(F32)).astype(BF16)


def fold(both):
    return both[:PROBES] + both[PROBES:]


def times(vecs, high, low):
    first = jnp.dot(vecs, high, preferred_element_type=F32)
    return fold(first) + jnp.dot(vecs[:PROBES], low, preferred_element_type=F32)


def kernel(nb, nc, ls_hbm, feat_hbm, vec_hbm, noise_hbm, signal_hbm, out_ref, lengthscales, noise, signal, rowbuf, colbuf, rows_t, row_vecs, cols,
           col_vecs, row_acc, col_acc, row_parts, col_parts, dist0, dist1, high0, high1, low0, low1,
           high_t0, high_t1, low_t0, low_t1, tall0, tall1,
           in_sem, row_send, row_recv, relay_send, relay_recv, col_send, col_recv, rp_send, rp_recv, cp_send, cp_recv):
    half = nb // 2
    pairs, chunks, ring = half // 2, nc // 2, nc // 2
    dist, highs, lows = (dist0, dist1), (high0, high1), (low0, low1)
    highs_t, lows_t = (high_t0, high_t1), (low_t0, low_t1)
    tall = (tall0, tall1)
    blk, col = lax.axis_index("blk"), lax.axis_index("col")
    core = blk % 2
    group, chip = blk - core + col % 2, col // 2

    def device(group, chip, core):
        return (group - group % 2 + core, 2 * chip + group % 2)

    own = colbuf.at[half]
    loads = [
        pltpu.make_async_copy(ls_hbm, lengthscales, in_sem.at[0]),
        pltpu.make_async_copy(feat_hbm, own.at[:FEAT], in_sem.at[1]),
        pltpu.make_async_copy(vec_hbm, own.at[FEAT:], in_sem.at[2]),
        pltpu.make_async_copy(noise_hbm, noise, in_sem.at[3]),
        pltpu.make_async_copy(signal_hbm, signal, in_sem.at[4]),
    ]
    for load in loads:
        load.start()

    def loop(first, last, action):
        def body(step, carry):
            action(step)
            return carry
        lax.fori_loop(first, last, body, 0)

    def row_offset(step):
        return (step + 1) // 2 if step % 2 else ring - step // 2

    def row_peer(step, other=False):
        return device(group, (chip + row_offset(step)) % ring, 1 - core if other else core)

    def row_owner(step, other):
        return device(group, (chip + ring - row_offset(step)) % ring, 1 - core if other else core)

    def col_offset(place):
        return nb - ORDER[place] if place % 2 else ORDER[place]

    def col_peer(place):
        return device((group + col_offset(place)) % nb, chip, core)

    def col_owner(place):
        return device((group + nb - col_offset(place)) % nb, chip, core)

    sibling = device(group, chip, 1 - core)
    barrier = pltpu.get_barrier_semaphore()

    def greet(peer):
        pl.semaphore_signal(barrier, inc=1, device_id=peer, device_id_type=MESH)

    for step in range(ring):
        if step:
            greet(row_owner(step, False))
        if step < ring // 2:
            greet(row_owner(step, True))
    for place in range(half):
        greet(col_owner(place))

    row_acc[...] = jnp.zeros_like(row_acc)
    col_acc[...] = jnp.zeros_like(col_acc)
    cols[DEPTH:, :] = jnp.zeros((WIDTH - DEPTH, cols.shape[1]), BF16)
    for load in loads:
        load.wait()
    feature = lax.broadcasted_iota(jnp.int32, (FEAT, WIDTH), 0)
    lengths = jnp.full((FEAT, WIDTH), lengthscales[0], F32)
    for k in range(1, FEAT):
        lengths = jnp.where(feature == k, lengthscales[k], lengths)
    own[:FEAT] = own[:FEAT] / lengths * SCALE
    rowbuf[0, 0] = own[...]
    for buffer in (high1, low1, high_t1, low_t1):
        buffer[...] = jnp.zeros_like(buffer)
    pl.semaphore_wait(barrier, ring - 1 + ring // 2 + half)

    def push(source, target, send, recv, device):
        return pltpu.make_async_remote_copy(
            src_ref=source, dst_ref=target, send_sem=send, recv_sem=recv, device_id=device, device_id_type=MESH)

    def row_copy(step):
        return push(own, rowbuf.at[0, step], row_send, row_recv.at[step], row_peer(step))

    def row_cross(step):
        if step < ring // 2:
            return push(own, rowbuf.at[1, step], relay_send, relay_recv.at[0], row_peer(step, True))
        return push(rowbuf.at[0, step], rowbuf.at[1, step], relay_send, relay_recv.at[1], sibling)

    def col_copy(place):
        return push(own, colbuf.at[place], col_send, col_recv.at[place // 2], col_peer(place))

    def row_part(slot):
        return push(row_acc.at[slot], row_parts.at[slot - 1], rp_send, rp_recv, row_owner(slot // 2, slot % 2))

    def col_part(place):
        return push(col_acc.at[place], col_parts.at[place], cp_send, cp_recv, col_owner(place))

    def await_all(region, sem):
        pltpu.make_async_copy(region, region, sem).wait()

    for step in range(ring // 2):
        if step:
            row_copy(step).start()
        row_cross(step).start()
    for place in range(half // 2):
        col_copy(place).start()
    for step in range(ring // 2, ring):
        row_copy(step).start()
    for place in range(half // 2, half):
        col_copy(place).start()

    def span(place, count):
        return pl.ds(pl.multiple_of(place * WIDTH, WIDTH), count * WIDTH)

    def put_col(place):
        block = colbuf[place]
        at = span(place, 1)
        cols[:DEPTH, at] = col_side(block[:FEAT]).astype(BF16)
        high, low = halves(block[FEAT:])
        col_vecs[:PROBES, at] = high
        col_vecs[PROBES:, at] = low

    def get_pair(pair):
        await_all(colbuf.at[pl.ds(2 * pair, 2)], col_recv.at[pair])
        put_col(2 * pair)
        put_col(2 * pair + 1)

    def pass_rows():
        for step in range(ring // 2, ring):
            await_all(rowbuf.at[0, step], row_recv.at[step])
            row_cross(step).start()

    def get_rows(side):
        first = side * ring // 2
        if side == 0:
            for step in range(1, ring // 2):
                await_all(rowbuf.at[0, step], row_recv.at[step])
        await_all(rowbuf.at[1, first:first + ring // 2], relay_recv.at[side])
        for slot in range(2 * first, 2 * first + ring):
            at = slice(slot * WIDTH, (slot + 1) * WIDTH)
            block = rowbuf.at[slot % 2, slot // 2]
            tall = jnp.concatenate([row_side(block[:FEAT]), jnp.zeros((WIDTH - DEPTH, WIDTH), F32)], axis=0)
            rows_t[at, :] = tall.T.astype(BF16)
            high, low = halves(block[FEAT:])
            row_vecs[:PROBES, at] = high
            row_vecs[PROBES:, at] = low

    def inner(slot, place, even):
        dist[even][...] = jnp.dot(rows_t[span(slot, 2), :], cols[:, span(place, 2)], preferred_element_type=F32)

    def elementwise(even):
        high, low = halves(matern(dist[even][...]))
        highs[even][...] = high
        lows[even][...] = low
        highs_t[even][...] = high.T
        lows_t[even][...] = low.T

    def add_rows(slot, place, even):
        total = times(col_vecs[:, span(place, 2)], highs_t[even][...], lows_t[even][...])
        for k in range(2):
            row_acc[slot + k] += total[:, k * WIDTH:(k + 1) * WIDTH]

    def add_cols(slot, place, even):
        total = times(row_vecs[:, span(slot, 2)], highs[even][...], lows[even][...])
        for k in range(2):
            col_acc[place + k] += total[:, k * WIDTH:(k + 1) * WIDTH]

    quarter, tiles = pairs // 2, nc // 4

    def unit_rows(unit):
        return jnp.where((unit >= quarter) & (unit < 3 * quarter), nc // 2, 0)

    def unit_place(unit):
        return 2 * jnp.where(unit < quarter, unit, jnp.where(unit < 3 * quarter, unit - quarter, unit - 2 * quarter))

    put_col(half)
    get_rows(0)
    get_pair(0)
    inner(0, 0, 0)

    def units(first, count):
        for step in range(count):
            unit = first + step
            slots, place = unit_rows(unit), unit_place(unit)
            next_slots, next_place = unit_rows(unit + 1), unit_place(jnp.minimum(unit + 1, 4 * quarter - 1))
            old = jnp.maximum(unit - 1, 0)
            old_slots, old_place = unit_rows(old), unit_place(old)
            for tile in range(tiles):
                even, odd = tile % 2, (tile + 1) % 2
                if tile + 1 < tiles:
                    inner(slots + 2 * tile + 2, place, odd)
                else:
                    inner(next_slots, next_place, odd)
                elementwise(even)
                if tile > 0:
                    add_cols(slots + 2 * tile - 2, place, odd)
                    add_rows(slots + 2 * tile - 2, place, odd)
                else:
                    add_cols(old_slots + 2 * tiles - 2, old_place, odd)
                    add_rows(old_slots + 2 * tiles - 2, old_place, odd)

    def send_cols(*ready):
        for pair in ready:
            col_part(2 * pair).start()
            col_part(2 * pair + 1).start()

    def early(unit):
        @pl.when(unit < quarter - 1)
        def _():
            get_pair(unit + 1)

        @pl.when(unit == 1)
        def _():
            pass_rows()

        @pl.when(unit == quarter - 1)
        def _():
            get_rows(1)
        units(unit, 1)

    def late(step):
        first = quarter + 2 * step

        @pl.when(first == 6)
        def _():
            get_pair(4)
            get_pair(5)

        @pl.when(first == 8)
        def _():
            get_pair(6)
            get_pair(7)
        units(first, 2)

        for when, ready in ((4, (0,)), (6, (1, 2)), (8, (3,)), (12, (4,)), (14, (5, 6))):
            @pl.when(first == when)
            def _():
                send_cols(*ready)
                if when == 12:
                    for slot in range(nc // 2, nc):
                        row_part(slot).start()

    loop(0, quarter, early)
    loop(0, 3 * quarter // 2, late)
    def own_inner(tile):
        tall[tile % 2][...] = jnp.dot(
            rows_t[span(4 * tile, 4), :], cols[:, span(half, 1)], preferred_element_type=F32)

    own_inner(0)
    add_cols(nc // 2 - 2, half - 2, 1)
    add_rows(nc // 2 - 2, half - 2, 1)
    col_part(half - 2).start()
    for slot in range(1, nc // 2):
        row_part(slot).start()
    total = row_acc[0]
    for tile in range(tiles):
        if tile + 1 < tiles:
            own_inner(tile + 1)
        high, low = halves(matern(tall[tile % 2][...]))
        total += times(row_vecs[:, span(4 * tile, 4)], high, low)

    await_all(col_parts, cp_recv)
    for place in range(half - 1):
        total += col_parts[place]
    await_all(row_parts, rp_recv)
    for slot in range(nc - 1):
        total += row_parts[slot]
    out_ref[...] = signal[0] * total + noise[...] * own[FEAT:]
    await_all(rowbuf.at[0, 1:], row_send)
    await_all(rowbuf.at[1], relay_send)
    await_all(colbuf.at[:half], col_send)
    await_all(row_parts, rp_send)
    await_all(col_parts, cp_send)


def on_device(nb, nc, features, vectors, lengthscales, noise_var, signal):
    half = nb // 2
    return pl.pallas_call(
        functools.partial(kernel, nb, nc),
        out_shape=jax.ShapeDtypeStruct((PROBES, WIDTH), F32),
        in_specs=[pl.BlockSpec(memory_space=pltpu.MemorySpace.HBM)] * 5,
        out_specs=pl.BlockSpec(memory_space=pltpu.VMEM),
        scratch_shapes=[
            pltpu.SMEM((FEAT,), F32),
            pltpu.VMEM((1, WIDTH), F32),
            pltpu.SMEM((1,), F32),
            pltpu.VMEM((2, nc // 2, FEAT + PROBES, WIDTH), F32),
            pltpu.VMEM((half + 1, FEAT + PROBES, WIDTH), F32),
            pltpu.VMEM((nc * WIDTH, WIDTH), BF16),
            pltpu.VMEM((2 * PROBES, nc * WIDTH), BF16),
            pltpu.VMEM((WIDTH, (half + 1) * WIDTH), BF16),
            pltpu.VMEM((2 * PROBES, (half + 1) * WIDTH), BF16),
            pltpu.VMEM((nc, PROBES, WIDTH), F32),
            pltpu.VMEM((half, PROBES, WIDTH), F32),
            pltpu.VMEM((nc - 1, PROBES, WIDTH), F32),
            pltpu.VMEM((half - 1, PROBES, WIDTH), F32),
        ]
        + [pltpu.VMEM((2 * WIDTH, 2 * WIDTH), F32)] * 2
        + [pltpu.VMEM((2 * WIDTH, 2 * WIDTH), BF16)] * 8
        + [pltpu.VMEM((4 * WIDTH, WIDTH), F32)] * 2
        + [
            pltpu.SemaphoreType.DMA((5,)),
            pltpu.SemaphoreType.DMA,
            pltpu.SemaphoreType.DMA((nc // 2,)),
            pltpu.SemaphoreType.DMA,
            pltpu.SemaphoreType.DMA((2,)),
            pltpu.SemaphoreType.DMA,
            pltpu.SemaphoreType.DMA((half // 2,)),
        ]
        + [pltpu.SemaphoreType.DMA] * 4,
        compiler_params=pltpu.CompilerParams(
            collective_id=0, has_side_effects=True, vmem_limit_bytes=60 * 1024 * 1024
        ),
        name="matern_sums",
    )(lengthscales, features, vectors, noise_var.reshape(1, WIDTH), signal)


def solution(mesh):
    nb, nc = mesh.shape["blk"], mesh.shape["col"]
    assert (nb, nc) == (2 * len(ORDER), 16)
    placed = (P(None, ("blk", "col")), P(None, ("blk", "col")), P(), P(("blk", "col")), P())
    return jax.shard_map(
        functools.partial(on_device, nb, nc),
        mesh=mesh,
        in_specs=placed,
        out_specs=P(None, ("blk", "col")),
        check_vma=False,
    )
```

time: 41.2 us -> 40.4 us (0.981)
  other arithmetic: 1.3 us -> 0 us
  local copies, waits for them, and re-layouts: 0.01 us -> 1.3 us
  Pallas kernels: 38.9 us -> 38.3 us
    add x1 -> x0, other arithmetic: 1.3 us -> none  [on_device(): return signal[0] * sums + noise_var[None, :] * vectors]
    unnamed x4 -> x1, local copies, waits for them, and re-layouts: 0.01 us -> 1.3 us
    pallas_call x1, Pallas kernels: 38.9 us -> 38.3 us  [on_device(): pl.pallas_call(functools.partial(kernel, nb, nc), out_shape=jax.ShapeDtyp...]
where the time goes in v4:
time: 40.4 us; the launch traced here: 40.2 us
  Pallas kernels  38.3 us (95%)
  local copies, waits for them, and re-layouts  1.3 us (3%)
  between operations  0.66 us (2%)
    pallas_call x1, Pallas kernels, on_device(): pl.pallas_call(functools.partial(kernel, nb, nc), out_shape=jax.ShapeDtyp...  38.3 us
    unnamed x1, local copies, waits for them, and re-layouts  1.3 us

profile of v4, /device:TPU:1, one launch (start us, length us, event | category | flops | bytes accessed | tf_op | source)
XLA Modules:
  0.0 40.2 jit_solution(10447963656890803646)
XLA Ops:
  0.7 38.3 %matern_sums.1 = f32[16,128]{1,0:T(8,128)} custom-call(f32[8]{0:T(128)} %ls_hbm.1, f32[8,128]{1,0:T(8,128)} %feat_hbm.1, f32[16,128]{1,0:T(8,128)} %vec_hbm.1, f32[1,128]{1,0:T(1,128)} %bitcast.1, f32[1]{0:T(128)S(6)} %copy.7.signal_hbm), custom_call_target="tpu_custom_call" | custom-call | tf_op jit(solution)/shard_map/matern_sums/pallas_call | solution.py:357
  38.9 1.3 %copy.8 = f32[16,128]{1,0:T(8,128)} copy(f32[16,128]{1,0:T(8,128)} %matern_sums.1) | data formatting | bytes 16384

commit v5 on v4

--- a/solution.py
+++ b/solution.py
@@ -107,16 +107,25 @@
         lax.fori_loop(first, last, body, 0)
 
     def row_offset(step):
-        return (step + 1) // 2 if step % 2 else ring - step // 2
+        if isinstance(step, int):
+            return (step + 1) // 2 if step % 2 else ring - step // 2
+        return jnp.where(step % 2 == 1, (step + 1) // 2, ring - step // 2)
 
     def row_peer(step, other=False):
         return device(group, (chip + row_offset(step)) % ring, 1 - core if other else core)
 
     def row_owner(step, other):
-        return device(group, (chip + ring - row_offset(step)) % ring, 1 - core if other else core)
+        return device(group, (chip + ring - row_offset(step)) % ring, (core + other) % 2)
+
+    offsets = [nb - far if place % 2 else far for place, far in enumerate(ORDER)]
 
     def col_offset(place):
-        return nb - ORDER[place] if place % 2 else ORDER[place]
+        if isinstance(place, int):
+            return offsets[place]
+        offset = offsets[0]
+        for k in range(1, half):
+            offset = jnp.where(place == k, offsets[k], offset)
+        return offset
 
     def col_peer(place):
         return device((group + col_offset(place)) % nb, chip, core)
@@ -132,9 +141,9 @@
 
     for step in range(ring):
         if step:
-            greet(row_owner(step, False))
+            greet(row_owner(step, 0))
         if step < ring // 2:
-            greet(row_owner(step, True))
+            greet(row_owner(step, 1))
     for place in range(half):
         greet(col_owner(place))
 
@@ -278,11 +287,6 @@
                     add_cols(old_slots + 2 * tiles - 2, old_place, odd)
                     add_rows(old_slots + 2 * tiles - 2, old_place, odd)
 
-    def send_cols(*ready):
-        for pair in ready:
-            col_part(2 * pair).start()
-            col_part(2 * pair + 1).start()
-
     def early(unit):
         @pl.when(unit < quarter - 1)
         def _():
@@ -311,13 +315,13 @@
             get_pair(7)
         units(first, 2)
 
-        for when, ready in ((4, (0,)), (6, (1, 2)), (8, (3,)), (12, (4,)), (14, (5, 6))):
-            @pl.when(first == when)
-            def _():
-                send_cols(*ready)
-                if when == 12:
-                    for slot in range(nc // 2, nc):
-                        row_part(slot).start()
+        whole = {2: 0, 4: 1, 6: 3, 8: 4, 10: 4, 12: 5, 14: 7}
+        start = stop = 0
+        for now in range(4, 16, 2):
+            start = jnp.where(first == now, 2 * whole[now - 2], start)
+            stop = jnp.where(first == now, 2 * whole[now], stop)
+        loop(start, stop, lambda place: col_part(place).start())
+        loop(nc // 2, jnp.where(first == 12, nc, nc // 2), lambda slot: row_part(slot).start())
 
     loop(0, quarter, early)
     loop(0, 3 * quarter // 2, late)
@@ -356,7 +360,7 @@
     half = nb // 2
     return pl.pallas_call(
         functools.partial(kernel, nb, nc),
-        out_shape=jax.ShapeDtypeStruct((PROBES, WIDTH), F32),
+        out_shape=pltpu.VMEM((PROBES, WIDTH), F32),
         in_specs=[pl.BlockSpec(memory_space=pltpu.MemorySpace.HBM)] * 5,
         out_specs=pl.BlockSpec(memory_space=pltpu.VMEM),
         scratch_shapes=[

time: 40.4 us -> 39 us (0.965)
  Pallas kernels: 38.3 us -> 37.5 us
  local copies, waits for them, and re-layouts: 1.3 us -> 0.6 us
    pallas_call x1, Pallas kernels: 38.3 us -> 37.5 us  [on_device(): pl.pallas_call(functools.partial(kernel, nb, nc), out_shape=pltpu.VMEM((P...]
    unnamed x1, local copies, waits for them, and re-layouts: 1.3 us -> 0.6 us
where the time goes in v5:
time: 39 us; the launch traced here: 38.8 us
  Pallas kernels  37.5 us (96%)
  between operations  0.66 us (2%)
  local copies, waits for them, and re-layouts  0.6 us (2%)
    pallas_call x1, Pallas kernels, on_device(): pl.pallas_call(functools.partial(kernel, nb, nc), out_shape=pltpu.VMEM((P...  37.5 us

profile of v5, /device:TPU:1, one launch (start us, length us, event | category | flops | bytes accessed | tf_op | source)
XLA Modules:
  0.0 38.8 jit_solution(3623508268539236077)
XLA Ops:
  0.7 37.5 %matern_sums.1 = f32[16,128]{1,0:T(8,128)S(1)} custom-call(f32[8]{0:T(128)} %ls_hbm.1, f32[8,128]{1,0:T(8,128)} %feat_hbm.1, f32[16,128]{1,0:T(8,128)} %vec_hbm.1, f32[1,128]{1,0:T(1,128)} %bitcast.1, f32[1]{0:T(128)S(6)} %copy.8.signal_hbm), custom_call_target="tpu_custom_call" | custom-call | tf_op jit(solution)/shard_map/matern_sums/pallas_call | solution.py:361
  38.2 0.6 %copy.7 = f32[16,128]{1,0:T(8,128)} copy(f32[16,128]{1,0:T(8,128)S(1)} %matern_sums.1) | data formatting | bytes 16384

commit v6 on v5

--- a/solution.py
+++ b/solution.py
@@ -139,13 +139,13 @@
     def greet(peer):
         pl.semaphore_signal(barrier, inc=1, device_id=peer, device_id_type=MESH)
 
-    for step in range(ring):
+    for place in reversed(range(half)):
+        greet(col_owner(place))
+    for step in reversed(range(ring)):
         if step:
             greet(row_owner(step, 0))
         if step < ring // 2:
             greet(row_owner(step, 1))
-    for place in range(half):
-        greet(col_owner(place))
 
     row_acc[...] = jnp.zeros_like(row_acc)
     col_acc[...] = jnp.zeros_like(col_acc)

time: 39 us -> 38.5 us (0.987)
  Pallas kernels: 37.5 us -> 37 us
    pallas_call x1, Pallas kernels: 37.5 us -> 37 us  [on_device(): pl.pallas_call(functools.partial(kernel, nb, nc), out_shape=pltpu.VMEM((P...]
where the time goes in v6:
time: 38.5 us; the launch traced here: 38.3 us
  Pallas kernels  37 us (96%)
  between operations  0.66 us (2%)
  local copies, waits for them, and re-layouts  0.6 us (2%)
    pallas_call x1, Pallas kernels, on_device(): pl.pallas_call(functools.partial(kernel, nb, nc), out_shape=pltpu.VMEM((P...  37 us

profile of v6, /device:TPU:1, one launch (start us, length us, event | category | flops | bytes accessed | tf_op | source)
XLA Modules:
  0.0 38.3 jit_solution(11911761608592041476)
XLA Ops:
  0.7 37.0 %matern_sums.1 = f32[16,128]{1,0:T(8,128)S(1)} custom-call(f32[8]{0:T(128)} %ls_hbm.1, f32[8,128]{1,0:T(8,128)} %feat_hbm.1, f32[16,128]{1,0:T(8,128)} %vec_hbm.1, f32[1,128]{1,0:T(1,128)} %bitcast.1, f32[1]{0:T(128)S(6)} %copy.8.signal_hbm), custom_call_target="tpu_custom_call" | custom-call | tf_op jit(solution)/shard_map/matern_sums/pallas_call | solution.py:361
  37.7 0.6 %copy.7 = f32[16,128]{1,0:T(8,128)} copy(f32[16,128]{1,0:T(8,128)S(1)} %matern_sums.1) | data formatting | bytes 16384

commit v7 on v6

--- a/solution.py
+++ b/solution.py
@@ -144,8 +144,7 @@
     for step in reversed(range(ring)):
         if step:
             greet(row_owner(step, 0))
-        if step < ring // 2:
-            greet(row_owner(step, 1))
+        greet(row_owner(step, 1))
 
     row_acc[...] = jnp.zeros_like(row_acc)
     col_acc[...] = jnp.zeros_like(col_acc)
@@ -160,7 +159,7 @@
     rowbuf[0, 0] = own[...]
     for buffer in (high1, low1, high_t1, low_t1):
         buffer[...] = jnp.zeros_like(buffer)
-    pl.semaphore_wait(barrier, ring - 1 + ring // 2 + half)
+    pl.semaphore_wait(barrier, ring - 1 + ring + half)
 
     def push(source, target, send, recv, device):
         return pltpu.make_async_remote_copy(
@@ -170,9 +169,7 @@
         return push(own, rowbuf.at[0, step], row_send, row_recv.at[step], row_peer(step))
 
     def row_cross(step):
-        if step < ring // 2:
-            return push(own, rowbuf.at[1, step], relay_send, relay_recv.at[0], row_peer(step, True))
-        return push(rowbuf.at[0, step], rowbuf.at[1, step], relay_send, relay_recv.at[1], sibling)
+        return push(own, rowbuf.at[1, step], relay_send, relay_recv.at[step // (ring // 2)], row_peer(step, True))
 
     def col_copy(place):
         return push(own, colbuf.at[place], col_send, col_recv.at[place // 2], col_peer(place))
@@ -194,6 +191,7 @@
         col_copy(place).start()
     for step in range(ring // 2, ring):
         row_copy(step).start()
+        row_cross(step).start()
     for place in range(half // 2, half):
         col_copy(place).start()
 
@@ -213,16 +211,10 @@
         put_col(2 * pair)
         put_col(2 * pair + 1)
 
-    def pass_rows():
-        for step in range(ring // 2, ring):
-            await_all(rowbuf.at[0, step], row_recv.at[step])
-            row_cross(step).start()
-
     def get_rows(side):
         first = side * ring // 2
-        if side == 0:
-            for step in range(1, ring // 2):
-                await_all(rowbuf.at[0, step], row_recv.at[step])
+        for step in range(max(first, 1), first + ring // 2):
+            await_all(rowbuf.at[0, step], row_recv.at[step])
         await_all(rowbuf.at[1, first:first + ring // 2], relay_recv.at[side])
         for slot in range(2 * first, 2 * first + ring):
             at = slice(slot * WIDTH, (slot + 1) * WIDTH)
@@ -291,10 +283,6 @@
         @pl.when(unit < quarter - 1)
         def _():
             get_pair(unit + 1)
-
-        @pl.when(unit == 1)
-        def _():
-            pass_rows()
 
         @pl.when(unit == quarter - 1)
         def _():

time: 38.5 us -> 38.8 us (level)
  Pallas kernels: 37 us -> 37.4 us
where the time goes in v7:
time: 38.8 us; the launch traced here: 38.7 us
  Pallas kernels  37.4 us (96%)
  between operations  0.66 us (2%)
  local copies, waits for them, and re-layouts  0.6 us (2%)
    pallas_call x1, Pallas kernels, on_device(): pl.pallas_call(functools.partial(kernel, nb, nc), out_shape=pltpu.VMEM((P...  37.4 us

profile of v7, /device:TPU:1, one launch (start us, length us, event | category | flops | bytes accessed | tf_op | source)
XLA Modules:
  0.0 38.7 jit_solution(9359295931471254410)
XLA Ops:
  0.7 37.4 %matern_sums.1 = f32[16,128]{1,0:T(8,128)S(1)} custom-call(f32[8]{0:T(128)} %ls_hbm.1, f32[8,128]{1,0:T(8,128)} %feat_hbm.1, f32[16,128]{1,0:T(8,128)} %vec_hbm.1, f32[1,128]{1,0:T(1,128)} %bitcast.1, f32[1]{0:T(128)S(6)} %copy.8.signal_hbm), custom_call_target="tpu_custom_call" | custom-call | tf_op jit(solution)/shard_map/matern_sums/pallas_call | solution.py:349
  38.1 0.6 %copy.7 = f32[16,128]{1,0:T(8,128)} copy(f32[16,128]{1,0:T(8,128)S(1)} %matern_sums.1) | data formatting | bytes 16384
